TPU v7x, 128 devices: a whole 4x4x4 slice. The times are simulated.
128 devices in a mesh: grp: 8 (over x, core), dev: 16 (over y, z).
Axes of the slice: x: 4, y: 4, z: 4, core: 2. Of those that a mesh axis runs over, the one named last changes fastest.
Arguments:
- features: bfloat16 [2, 131072, 256], P(None, ('grp', 'dev')), may hold values from -6 to 6
- w_source: bfloat16 [256, 256], P('dev'), may hold values from -0.375 to 0.375
- w_target: bfloat16 [256, 256], P('dev'), may hold values from -0.375 to 0.375
- w_residual: bfloat16 [256, 256], P('dev'), may hold values from -0.375 to 0.375
- attention: bfloat16 [256], P('dev'), may hold values from -1.5 to 1.5
- out_bias: bfloat16 [256], P('dev'), may hold values from -3 to 3
- norm_gain: bfloat16 [256], P('dev'), may hold values from 0.5 to 1.5
- norm_shift: bfloat16 [256], P('dev'), may hold values from -1.796875 to 1.796875
- node_count: int32 [2, 128], P(None, ('grp', 'dev')), may hold values from 512 to 1024, as said below
- edge_src: int32 [2, 128, 128, 16], P(None, ('grp', 'dev')), may hold values from 0 to 1023, as said below
- edge_tgt: int32 [2, 128, 128, 16], P(None, ('grp', 'dev')), may hold values from -1 to 1023, as said below
- cotangent: bfloat16 [2, 131072, 256], P(None, ('grp', 'dev')), may hold values from -6 to 6
Outputs:
- output: bfloat16 [2, 131072, 256], P(None, ('grp', 'dev'))
- grad_features: bfloat16 [2, 131072, 256], P(None, ('grp', 'dev'))
- grad_w_source: float32 [256, 256], P('dev')
- grad_w_target: float32 [256, 256], P('dev')
- grad_w_residual: float32 [256, 256], P('dev')
- grad_attention: float32 [256], P('dev')
- grad_bias: float32 [256], P('dev')
- grad_gain: float32 [256], P('dev')
- grad_shift: float32 [256], P('dev')
Inputs may be any that keep to these rules, and one draw needn't show every extreme that they name: `node_count`: in each micro-batch some device holds exactly 1024 live nodes. `edge_src`: entry [b, s, t, k] is below node_count[b, s]. `edge_tgt`: entry [b, t, s, k] is below node_count[b, t] for the first c slots, where c from s to t is 8 to 16 (each source device sends exactly 16 to some target device in each micro-batch), and -1 in the others.
All inputs are finite; a program needn't handle non-finite values.
Results may differ from a plain program's by a relative error of at most 0.0075.
Values may be sent and summed in bfloat16 or wider, within the bound.
A program may use at most 128 MiB of HBM per device.

v0:
```python
import jax
import jax.numpy as jnp
from jax import lax
from jax.sharding import PartitionSpec as P

H = 4


def smooth_unit(value):
    return jax.nn.gelu(value, approximate=True)


def times_trans(left, right):
    return lax.dot_general(
        left, right, (((1,), (1,)), ((), ())), preferred_element_type=jnp.float32
    )


def trans_times(left, right):
    return lax.dot_general(
        left, right, (((0,), (0,)), ((), ())), preferred_element_type=jnp.float32
    )


def pick_rows(onehot, table):
    return jnp.dot(onehot, table, precision=lax.Precision.HIGH, preferred_element_type=jnp.float32)


def spread_rows(onehot, values):
    return lax.dot_general(
        onehot,
        values,
        (((0,), (0,)), ((), ())),
        precision=lax.Precision.HIGH,
        preferred_element_type=jnp.float32,
    )


def send_rows(buffer):
    return lax.all_to_all(buffer, ("grp", "dev"), split_axis=0, concat_axis=0, tiled=True)


def return_rows(buffer):
    return lax.all_to_all(buffer, ("grp", "dev"), split_axis=0, concat_axis=0, tiled=True)


def one_batch(rows, upstream, live_count, src_index, tgt_index, weights):
    wsrc, wtgt, wres, attn_vec, bias_vec, gain_vec, shift_vec = weights
    count_nodes, width = rows.shape
    head_width = width // H
    attn_heads = attn_vec.astype(jnp.float32).reshape(H, head_width)
    bias_f = bias_vec.astype(jnp.float32)
    gain_f = gain_vec.astype(jnp.float32)
    shift_f = shift_vec.astype(jnp.float32)
    node_ids = jnp.arange(count_nodes, dtype=jnp.int32)
    node_live = (node_ids < live_count)[:, None].astype(jnp.float32)
    src_proj = jnp.dot(rows, wsrc, preferred_element_type=jnp.float32).astype(jnp.bfloat16)
    tgt_proj = jnp.dot(rows, wtgt, preferred_element_type=jnp.float32)
    res_proj = jnp.dot(rows, wres, preferred_element_type=jnp.float32)
    src_flat = src_index.reshape(-1)
    src_hot = (src_flat[:, None] == node_ids[None, :]).astype(jnp.bfloat16)
    outgoing = jnp.dot(src_hot, src_proj, preferred_element_type=jnp.float32).astype(jnp.bfloat16)
    outgoing = outgoing.reshape(src_index.shape + (width,))
    arrived = send_rows(outgoing)
    slot_shape = arrived.shape
    edge_rows = arrived.reshape(-1, width).astype(jnp.float32)
    flat_tgt = tgt_index.reshape(-1)
    tgt_match = flat_tgt[:, None] == node_ids[None, :]
    tgt_hot = tgt_match.astype(jnp.float32)
    edge_live = (flat_tgt >= 0)[:, None].astype(jnp.float32)
    edge_sum = edge_rows + pick_rows(tgt_hot, tgt_proj)
    edge_unit = smooth_unit(edge_sum).reshape(-1, H, head_width)
    edge_score = jnp.sum(edge_unit * attn_heads, axis=-1)
    src_f = src_proj.astype(jnp.float32)
    self_sum = src_f + tgt_proj
    self_unit = smooth_unit(self_sum).reshape(-1, H, head_width)
    self_score = jnp.sum(self_unit * attn_heads, axis=-1)
    node_match = jnp.transpose(tgt_match)
    tops = []
    for head in range(H):
        tops.append(jnp.max(jnp.where(node_match, edge_score[:, head][None, :], -jnp.inf), axis=1))
    edge_top = jnp.stack(tops, axis=-1)
    top_score = jnp.maximum(edge_top, self_score)
    edge_exp = jnp.exp(edge_score - pick_rows(tgt_hot, top_score)) * edge_live
    self_exp = jnp.exp(self_score - top_score)
    denom = spread_rows(tgt_hot, edge_exp) + self_exp
    edge_alpha = edge_exp / (pick_rows(tgt_hot, denom) + (1.0 - edge_live))
    self_alpha = self_exp / denom
    edge_heads = edge_rows.reshape(-1, H, head_width)
    src_heads = src_f.reshape(-1, H, head_width)
    aggregate = spread_rows(
        tgt_hot, (edge_alpha[:, :, None] * edge_heads).reshape(-1, width)
    ).reshape(-1, H, head_width)
    aggregate = aggregate + self_alpha[:, :, None] * src_heads
    summed = aggregate.reshape(-1, width) + bias_f + res_proj
    centre = summed - jnp.mean(summed, axis=-1, keepdims=True)
    inverse = lax.rsqrt(jnp.mean(centre * centre, axis=-1, keepdims=True) + 1e-05)
    normed = centre * inverse
    linear = normed * gain_f + shift_f
    result = (jax.nn.elu(linear) * node_live).astype(jnp.bfloat16)
    grad_out = upstream.astype(jnp.float32) * node_live
    grad_lin = grad_out * jnp.where(linear > 0, 1.0, jnp.exp(jnp.minimum(linear, 0.0)))
    grad_gain = jnp.sum(grad_lin * normed, axis=0)
    grad_shift = jnp.sum(grad_lin, axis=0)
    grad_norm = grad_lin * gain_f
    grad_pre = inverse * (
        grad_norm
        - jnp.mean(grad_norm, axis=-1, keepdims=True)
        - normed * jnp.mean(grad_norm * normed, axis=-1, keepdims=True)
    )
    grad_bias = jnp.sum(grad_pre, axis=0)
    grad_res = grad_pre.astype(jnp.bfloat16)
    grad_agg = grad_pre.reshape(-1, H, head_width)
    overall = jnp.sum(grad_agg * aggregate, axis=-1)
    edge_grad_agg = pick_rows(tgt_hot, grad_pre).reshape(-1, H, head_width)
    edge_dalpha = jnp.sum(edge_grad_agg * edge_heads, axis=-1)
    edge_dscore = edge_alpha * (edge_dalpha - pick_rows(tgt_hot, overall))
    self_dalpha = jnp.sum(grad_agg * src_heads, axis=-1)
    self_dscore = self_alpha * (self_dalpha - overall)
    grad_attn = jnp.sum(edge_dscore[:, :, None] * edge_unit, axis=0) + jnp.sum(
        self_dscore[:, :, None] * self_unit, axis=0
    )
    unused, edge_back = jax.vjp(smooth_unit, edge_sum)
    edge_dz = edge_back((edge_dscore[:, :, None] * attn_heads).reshape(-1, width))[0]
    unused_self, self_back = jax.vjp(smooth_unit, self_sum)
    self_dz = self_back((self_dscore[:, :, None] * attn_heads).reshape(-1, width))[0]
    edge_grad = (edge_alpha[:, :, None] * edge_grad_agg).reshape(-1, width) + edge_dz
    returned = return_rows(edge_grad.astype(jnp.bfloat16).reshape(slot_shape))
    grad_src = trans_times(src_hot, returned.reshape(-1, width))
    grad_src = grad_src + (self_alpha[:, :, None] * grad_agg).reshape(-1, width) + self_dz
    grad_src = grad_src.astype(jnp.bfloat16)
    grad_tgt = spread_rows(tgt_hot, edge_dz) + self_dz
    grad_tgt = grad_tgt.astype(jnp.bfloat16)
    grad_wsrc = trans_times(rows, grad_src)
    grad_wtgt = trans_times(rows, grad_tgt)
    grad_wres = trans_times(rows, grad_res)
    grad_rows = (
        times_trans(grad_src, wsrc) + times_trans(grad_tgt, wtgt) + times_trans(grad_res, wres)
    )
    terms = (
        grad_wsrc,
        grad_wtgt,
        grad_wres,
        grad_attn.reshape(width),
        grad_bias,
        grad_gain,
        grad_shift,
    )
    return (result, grad_rows.astype(jnp.bfloat16), terms)


def local(
    features,
    w_source,
    w_target,
    w_residual,
    attention,
    out_bias,
    norm_gain,
    norm_shift,
    node_count,
    edge_src,
    edge_tgt,
    cotangent,
):
    batches = features.shape[0]
    shards = (w_source, w_target, w_residual, attention, out_bias, norm_gain, norm_shift)
    shard_acc = tuple((jnp.zeros(piece.shape, jnp.float32) for piece in shards))
    results = []
    grad_list = []
    for batch in range(batches):
        weights = (
            lax.all_gather(w_source, "dev", axis=0, tiled=True),
            lax.all_gather(w_target, "dev", axis=0, tiled=True),
            lax.all_gather(w_residual, "dev", axis=0, tiled=True),
            lax.all_gather(attention, "dev", axis=0, tiled=True),
            lax.all_gather(out_bias, "dev", axis=0, tiled=True),
            lax.all_gather(norm_gain, "dev", axis=0, tiled=True),
            lax.all_gather(norm_shift, "dev", axis=0, tiled=True),
        )
        result, grad_rows, terms = one_batch(
            features[batch],
            cotangent[batch],
            node_count[batch, 0],
            edge_src[batch, 0],
            edge_tgt[batch, 0],
            weights,
        )
        results.append(result)
        grad_list.append(grad_rows)
        scattered = (
            lax.psum_scatter(terms[0], "dev", scatter_dimension=0, tiled=True),
            lax.psum_scatter(terms[1], "dev", scatter_dimension=0, tiled=True),
            lax.psum_scatter(terms[2], "dev", scatter_dimension=0, tiled=True),
            lax.psum_scatter(terms[3], "dev", scatter_dimension=0, tiled=True),
            lax.psum_scatter(terms[4], "dev", scatter_dimension=0, tiled=True),
            lax.psum_scatter(terms[5], "dev", scatter_dimension=0, tiled=True),
            lax.psum_scatter(terms[6], "dev", scatter_dimension=0, tiled=True),
        )
        summed = lax.psum(
            (
                scattered[0],
                scattered[1],
                scattered[2],
                scattered[3],
                scattered[4],
                scattered[5],
                scattered[6],
            ),
            "grp",
        )
        shard_acc = tuple((left + right for left, right in zip(shard_acc, summed)))
    return (
        jnp.stack(results),
        jnp.stack(grad_list),
        shard_acc[0],
        shard_acc[1],
        shard_acc[2],
        shard_acc[3],
        shard_acc[4],
        shard_acc[5],
        shard_acc[6],
    )


def solution(mesh):
    return jax.shard_map(
        local,
        mesh=mesh,
        in_specs=(
            P(None, ("grp", "dev"), None),
            P("dev", None),
            P("dev", None),
            P("dev", None),
            P("dev"),
            P("dev"),
            P("dev"),
            P("dev"),
            P(None, ("grp", "dev")),
            P(None, ("grp", "dev"), None, None),
            P(None, ("grp", "dev"), None, None),
            P(None, ("grp", "dev"), None),
        ),
        out_specs=(
            P(None, ("grp", "dev"), None),
            P(None, ("grp", "dev"), None),
            P("dev", None),
            P("dev", None),
            P("dev", None),
            P("dev"),
            P("dev"),
            P("dev"),
            P("dev"),
        ),
        check_vma=False,
    )
```

profile of v0, /device:TPU:1, one launch (start us, length us, event | category | flops | bytes accessed | tf_op | source)
XLA Modules:
  0.0 626.2 jit_solution(2517490388828414601)
XLA Ops:
  7.2 20.7 %all_gather.28 = bf16[256,256]{1,0:T(8,128)(2,1)S(1)} all-gather(bf16[16,256]{1,0:T(8,128)(2,1)} %param.13), channel_id=1, replica_groups=mesh['grp'=8,'dev'=16] {'dev'}, dimensions={0}, use_global_device_ids=true | all-gather | bytes 139264 | tf_op jit(solution)/shard_map/all_gather | solution.py:173
  33.7 12.8 %all-to-all-start = ((bf16[128,16,256]{2,1,0:T(8,128)(2,1)}), bf16[128,16,256]{2,1,0:T(8,128)(2,1)S(1)}, u32[]{:S(2)}, u32[]{:S(2)}) async-start(bf16[128,16,256]{2,1,0:T(8,128)(2,1)} %bitcast.255), calls=%async_computation | async-start | bytes 2097152 | tf_op jit(solution)/shard_map/all_to_all | solution.py:40
  50.3 34.9 %all-reduce.10 = (bf16[256]{0:T(256)(128)(2,1)S(1)}, bf16[256]{0:T(256)(128)(2,1)S(1)}, bf16[256]{0:T(256)(128)(2,1)S(1)}, bf16[256]{0:T(256)(128)(2,1)S(1)}) all-reduce(bf16[256]{0:T(256)(128)(2,1)S(1)} %dynamic-update-slice.3, bf16[256]{0:T(256)(128)(2,1)S(1)} %dynamic-update-slice.2, ...), channel_id=1, replica_groups=mesh['grp'=8,'dev'=16] {'dev'}, use_global_device_ids=true, to_apply=%add.3 | all-reduce | flops 1024 | bytes 4096
  87.0 15.4 %all_gather.29 = bf16[256,256]{1,0:T(8,128)(2,1)S(1)} all-gather(bf16[16,256]{1,0:T(8,128)(2,1)S(1)} %copy-done.55), channel_id=1, replica_groups=mesh['grp'=8,'dev'=16] {'dev'}, dimensions={0}, use_global_device_ids=true | all-gather | bytes 139264 | tf_op jit(solution)/shard_map/all_gather | solution.py:174
  118.8 20.1 %all-to-all-start.1 = ((bf16[128,16,256]{2,1,0:T(8,128)(2,1)}), bf16[128,16,256]{2,1,0:T(8,128)(2,1)S(1)}, u32[]{:S(2)}, u32[]{:S(2)}) async-start(bf16[128,16,256]{2,1,0:T(8,128)(2,1)} %bitcast.256), calls=%async_computation.1 | async-start | bytes 2097152 | tf_op jit(solution)/shard_map/all_to_all | solution.py:40
  139.0 23.8 %all_gather.32 = bf16[256,256]{1,0:T(8,128)(2,1)S(1)} all-gather(bf16[16,256]{1,0:T(8,128)(2,1)} %param.15), channel_id=1, replica_groups=mesh['grp'=8,'dev'=16] {'dev'}, dimensions={0}, use_global_device_ids=true | all-gather | bytes 139264 | tf_op jit(solution)/shard_map/all_gather | solution.py:175
  166.1 4.4 multiply_multiply_fusion.5
  175.1 4.4 multiply_multiply_fusion.4
  185.5 4.7 select_reduce_fusion.7
  209.1 4.7 select_reduce_fusion.3
  232.9 4.8 fusion.81
  244.9 3.8 fusion.175
  249.8 4.0 fusion.4
  254.8 3.8 fusion.14
  258.6 4.7 reshape.265
  263.3 4.8 copy.117
  282.6 4.0 fusion.122
  289.3 4.7 reshape.263
  293.9 4.8 copy.110
  311.8 5.8 multiply_reduce_fusion.1
  317.6 15.6 %all-to-all-start.2 = ((bf16[128,16,256]{2,1,0:T(8,128)(2,1)}), bf16[128,16,256]{2,1,0:T(8,128)(2,1)}, u32[]{:S(2)}, u32[]{:S(2)}) async-start(bf16[128,16,256]{2,1,0:T(8,128)(2,1)} %bitcast.250), calls=%async_computation.2 | async-start | bytes 2097152 | tf_op jit(solution)/shard_map/all_to_all | solution.py:44
  333.8 7.1 %fusion.93 = bf16[1024,256]{0,1:T(8,128)(2,1)S(1)} fusion(f32[1024,256]{0,1:T(8,128)} %get-tuple-element.97, s32[2048]{0:T(1024)S(1)} %eq.74, f32[2048,256]{1,0:T(8,128)} %get-tuple-element.126, f32[2048,256]{1,0:T(8,128)} %copy.111, f32[256]{0:T(256)} %convert_element_type.154), kind=kOutput, calls=%fused_computation.139 | convolution fusion | flops 3234332672 | bytes 5776384 | tf_op jit(solution)/shard_map/dot_general | solution.py:30
  341.7 4.4 fusion.91
  352.9 5.2 multiply_reduce_fusion
  360.9 10.2 %all-to-all-start.3 = ((bf16[128,16,256]{2,1,0:T(8,128)(2,1)}), bf16[128,16,256]{2,1,0:T(8,128)(2,1)}, u32[]{:S(2)}, u32[]{:S(2)}) async-start(bf16[128,16,256]{2,1,0:T(8,128)(2,1)} %bitcast.249), calls=%async_computation.3 | async-start | bytes 2097152 | tf_op jit(solution)/shard_map/all_to_all | solution.py:44
  378.8 34.7 %all-reduce.8 = (f32[256]{0:T(256)S(1)}, f32[256]{0:T(256)}, f32[256]{0:T(256)}, f32[256]{0:T(256)}) all-reduce(f32[256]{0:T(256)} %add_add_fusion, f32[256]{0:T(256)} %add.302, f32[256]{0:T(256)} %add.303, f32[256]{0:T(256)} %add.304), channel_id=12, replica_groups=mesh['grp'=8,'dev'=16] {'dev'}, use_global_device_ids=true, to_apply=%region_40.41.clone | all-reduce | flops 1024 | bytes 8192
  416.8 10.8 %reduce-scatter.12.cloned.1.call-done = f32[16,256]{1,0:T(8,128)} async-done(((f32[256,256]{1,0:T(8,128)}), f32[16,256]{1,0:T(8,128)}) %reduce-scatter.12.cloned.1.call-update) | async-done | bytes 16400
  429.1 73.3 %reduce-scatter.14.cloned.1.call-done = f32[16,256]{1,0:T(8,128)} async-done(((f32[256,256]{1,0:T(8,128)}), f32[16,256]{1,0:T(8,128)}) %reduce-scatter.14.cloned.1.call-update) | async-done | bytes 16400
  503.9 3.8 fusion.92
  510.1 3.9 fusion.90
  521.3 68.5 %reduce-scatter.10.cloned.1.call-done = f32[16,256]{1,0:T(8,128)} async-done(((f32[256,256]{1,0:T(8,128)}), f32[16,256]{1,0:T(8,128)}) %reduce-scatter.10.cloned.1.call-update) | async-done | bytes 16400
  590.7 26.8 %all-reduce.9 = (f32[16,256]{0,1:T(8,128)S(1)}, f32[16,256]{0,1:T(8,128)S(1)}, f32[16,256]{0,1:T(8,128)S(1)}, f32[16]{0:T(128)}, f32[16]{0:T(128)}, /*index=5*/f32[16]{0:T(128)}, f32[16]{0:T(128)}) all-reduce(f32[16,256]{0,1:T(8,128)S(1)} %copy.132, f32[16,256]{0,1:T(8,128)S(1)} %copy-done.29, ...), channel_id=1, replica_groups=mesh['grp'=8,'dev'=16] {'grp'}, use_global_device_ids=true, to_apply=%region_27.28 | all-reduce | flops 12352 | bytes 98816 | tf_op jit(solution)/shard_map/psum | solution.py:200
  (301 shorter events, 154.3 us)
Async XLA Ops:
  31.2 79.7 %copy-start.9 = (bf16[1024,256]{0,1:T(8,128)(2,1)}, bf16[1024,256]{0,1:T(8,128)(2,1)S(1)}, u32[]{:S(2)}) copy-start(bf16[1024,256]{0,1:T(8,128)(2,1)S(1)} %get-tuple-element.131) | copy-start | bytes 1572868
  33.7 12.9 %copy-start = (bf16[2,1024,256]{2,1,0:T(8,128)(2,1)S(1)}, bf16[2,1024,256]{2,1,0:T(8,128)(2,1)}, u32[]{:S(2)}) copy-start(bf16[2,1024,256]{2,1,0:T(8,128)(2,1)} %param.12) | copy-start | bytes 3145732
  33.7 14.3 %copy-start.75 = (u32[128]{0:T(128)S(1)}, u32[128]{0:T(128)}, u32[]{:S(2)}) copy-start(u32[128]{0:T(128)} %constant.52) | copy-start | bytes 1540
  33.7 15.6 %copy-start.80 = (bf16[16]{0:T(256)(128)(2,1)S(1)}, bf16[16]{0:T(256)(128)(2,1)}, u32[]{:S(2)}) copy-start(bf16[16]{0:T(256)(128)(2,1)} %param.19) | copy-start | bytes 100
  33.7 15.9 %copy-start.81 = (bf16[16]{0:T(256)(128)(2,1)S(1)}, bf16[16]{0:T(256)(128)(2,1)}, u32[]{:S(2)}) copy-start(bf16[16]{0:T(256)(128)(2,1)} %param.18) | copy-start | bytes 100
  33.7 16.1 %copy-start.82 = (bf16[16]{0:T(256)(128)(2,1)S(1)}, bf16[16]{0:T(256)(128)(2,1)}, u32[]{:S(2)}) copy-start(bf16[16]{0:T(256)(128)(2,1)} %param.16) | copy-start | bytes 100
  33.7 16.3 %copy-start.83 = (bf16[16]{0:T(256)(128)(2,1)S(1)}, bf16[16]{0:T(256)(128)(2,1)}, u32[]{:S(2)}) copy-start(bf16[16]{0:T(256)(128)(2,1)} %param.17) | copy-start | bytes 100
  33.7 53.3 %copy-start.55 = (bf16[16,256]{1,0:T(8,128)(2,1)S(1)}, bf16[16,256]{1,0:T(8,128)(2,1)}, u32[]{:S(2)}) copy-start(bf16[16,256]{1,0:T(8,128)(2,1)} %param.14) | copy-start | bytes 24580
  33.7 68.7 %copy-start.54 = (s32[2,1,128,16]{2,3,1,0:T(8,128)S(1)}, s32[2,1,128,16]{2,3,1,0:T(8,128)}, u32[]{:S(2)}) copy-start(s32[2,1,128,16]{2,3,1,0:T(8,128)} %param.22) | copy-start | bytes 49156
  33.7 85.1 %all-to-all-start = ((bf16[128,16,256]{2,1,0:T(8,128)(2,1)}), bf16[128,16,256]{2,1,0:T(8,128)(2,1)S(1)}, u32[]{:S(2)}, u32[]{:S(2)}) async-start(bf16[128,16,256]{2,1,0:T(8,128)(2,1)} %bitcast.255), calls=%async_computation | async-start | bytes 2097152 | tf_op jit(solution)/shard_map/all_to_all | solution.py:40
  47.9 68.4 %copy-start.11 = (bf16[1024,256]{0,1:T(8,128)(2,1)}, bf16[1024,256]{0,1:T(8,128)(2,1)S(1)}, u32[]{:S(2)}) copy-start(bf16[1024,256]{0,1:T(8,128)(2,1)S(1)} %get-tuple-element.135) | copy-start | bytes 1572868
  85.2 25.7 %copy-start.48 = (f32[4,64]{1,0:T(4,128)}, f32[4,64]{1,0:T(4,128)S(1)}, u32[]{:S(2)}) copy-start(f32[4,64]{1,0:T(4,128)S(1)} %mul.532) | copy-start | bytes 3076
  102.8 13.5 %copy-start.58 = (s32[2048]{0:T(1024)}, s32[2048]{0:T(1024)S(1)}, u32[]{:S(2)}) copy-start(s32[2048]{0:T(1024)S(1)} %eq.89) | copy-start | bytes 24580
  118.8 47.3 %copy-start.3 = (bf16[128,16,256]{2,1,0:T(8,128)(2,1)}, bf16[128,16,256]{2,1,0:T(8,128)(2,1)S(1)}, u32[]{:S(2)}) copy-start(bf16[128,16,256]{2,1,0:T(8,128)(2,1)S(1)} %all-to-all-done) | copy-start | bytes 3145732
  118.8 54.7 %all-to-all-start.1 = ((bf16[128,16,256]{2,1,0:T(8,128)(2,1)}), bf16[128,16,256]{2,1,0:T(8,128)(2,1)S(1)}, u32[]{:S(2)}, u32[]{:S(2)}) async-start(bf16[128,16,256]{2,1,0:T(8,128)(2,1)} %bitcast.256), calls=%async_computation.1 | async-start | bytes 2097152 | tf_op jit(solution)/shard_map/all_to_all | solution.py:40
  138.9 27.2 %copy-start.17 = (f32[1024,256]{0,1:T(8,128)S(1)}, f32[1024,256]{0,1:T(8,128)}, u32[]{:S(2)}) copy-start(f32[1024,256]{0,1:T(8,128)} %get-tuple-element.129) | copy-start | bytes 3145732
  184.8 11.0 %copy-start.31 = (f32[2048,4]{0,1:T(4,128)}, f32[2048,4]{0,1:T(4,128)S(1)}, u32[]{:S(2)}) copy-start(f32[2048,4]{0,1:T(4,128)S(1)} %get-tuple-element.72) | copy-start | bytes 98308
  206.0 7.8 %copy-start.32 = (f32[2048,4]{0,1:T(4,128)S(1)}, f32[2048,4]{0,1:T(4,128)}, u32[]{:S(2)}) copy-start(f32[2048,4]{0,1:T(4,128)} %copy-done.31) | copy-start | bytes 98308
  317.6 43.2 %all-to-all-start.2 = ((bf16[128,16,256]{2,1,0:T(8,128)(2,1)}), bf16[128,16,256]{2,1,0:T(8,128)(2,1)}, u32[]{:S(2)}, u32[]{:S(2)}) async-start(bf16[128,16,256]{2,1,0:T(8,128)(2,1)} %bitcast.250), calls=%async_computation.2 | async-start | bytes 2097152 | tf_op jit(solution)/shard_map/all_to_all | solution.py:44
  333.3 94.3 %reduce-scatter.12.cloned.1.call-start = ((), (), s32[]{:S(2)}) async-start(), calls=%async_computation.8 | async-start | bytes 278528
  333.7 7.9 %copy-start.7 = (f32[2048,256]{1,0:T(8,128)S(1)}, f32[2048,256]{1,0:T(8,128)}, u32[]{:S(2)}) copy-start(f32[2048,256]{1,0:T(8,128)} %copy.118) | copy-start | bytes 6291460
  333.7 7.9 %copy-start.21 = (f32[2048,256]{1,0:T(8,128)S(1)}, f32[2048,256]{1,0:T(8,128)}, u32[]{:S(2)}) copy-start(f32[2048,256]{1,0:T(8,128)} %get-tuple-element.128) | copy-start | bytes 6291460
  333.7 7.9 %copy-start.27 = (f32[1024,256]{0,1:T(8,128)S(1)}, f32[1024,256]{0,1:T(8,128)}, u32[]{:S(2)}) copy-start(f32[1024,256]{0,1:T(8,128)} %get-tuple-element.99) | copy-start | bytes 3145732
  333.8 7.9 %copy-start.52 = (f32[256]{0:T(256)S(1)}, f32[256]{0:T(256)}, u32[]{:S(2)}) copy-start(f32[256]{0:T(256)} %convert_element_type.154) | copy-start | bytes 3076
  349.7 152.7 %reduce-scatter.14.cloned.1.call-start = ((), (), s32[]{:S(2)}) async-start(), calls=%async_computation.9 | async-start | bytes 278528
  360.9 149.3 %all-to-all-start.3 = ((bf16[128,16,256]{2,1,0:T(8,128)(2,1)}), bf16[128,16,256]{2,1,0:T(8,128)(2,1)}, u32[]{:S(2)}, u32[]{:S(2)}) async-start(bf16[128,16,256]{2,1,0:T(8,128)(2,1)} %bitcast.249), calls=%async_computation.3 | async-start | bytes 2097152 | tf_op jit(solution)/shard_map/all_to_all | solution.py:44
  371.1 218.8 %reduce-scatter.10.cloned.1.call-start = ((), (), s32[]{:S(2)}) async-start(), calls=%async_computation.7 | async-start | bytes 278528
  371.2 132.7 %copy-start.57 = (s32[2048]{0:T(1024)S(1)}, s32[2048]{0:T(1024)}, u32[]{:S(2)}) copy-start(s32[2048]{0:T(1024)} %copy-done.56) | copy-start | bytes 24580
  519.9 70.8 %copy-start.29 = (f32[16,256]{0,1:T(8,128)S(1)}, f32[16,256]{0,1:T(8,128)}, u32[]{:S(2)}) copy-start(f32[16,256]{0,1:T(8,128)} %copy.134) | copy-start | bytes 49156
  519.9 70.8 %copy-start.30 = (f32[16,256]{0,1:T(8,128)S(1)}, f32[16,256]{0,1:T(8,128)}, u32[]{:S(2)}) copy-start(f32[16,256]{0,1:T(8,128)} %copy.136) | copy-start | bytes 49156
  519.9 70.8 %copy-start.78 = (f32[16]{0:T(128)S(1)}, f32[16]{0:T(128)}, u32[]{:S(2)}) copy-start(f32[16]{0:T(128)} %dynamic-slice.9) | copy-start | bytes 196
  519.9 70.8 %copy-start.79 = (f32[16]{0:T(128)S(1)}, f32[16]{0:T(128)}, u32[]{:S(2)}) copy-start(f32[16]{0:T(128)} %dynamic-slice.11) | copy-start | bytes 196
  (59 other events, 196.7 us)
Sparse Core Ops, SparseCore 0:
  349.8 77.7 reduce-scatter.11
  431.1 71.2 reduce-scatter.13
  518.4 71.3 reduce-scatter.9
where the time goes:
time: 637 us; the launch traced here: 626 us
  blocking collectives  156 us (24%)
  waiting for transfers between devices  153 us (24%)
  matrix products  89.5 us (14%)
  local copies, waits for them, and re-layouts  84.4 us (13%)
  other arithmetic  67.7 us (11%)
  starting transfers between devices  59.3 us (9%)
  between operations  16.4 us (3%)
    unnamed x6, waiting for transfers between devices  153 us
    unnamed x2, blocking collectives  69.6 us
    dot_general x10, matrix products, pick_rows(): jnp.dot(onehot, table, precision=lax.Precision.HIGH, preferred_element_ty...  34.1 us
    all_to_all x2, starting transfers between devices, send_rows(): lax.all_to_all(buffer, ('grp', 'dev'), split_axis=0, concat_axis=0, tiled...  32.9 us
    psum x1, blocking collectives, local(): lax.psum((scattered[0], scattered[1], scattered[2], scattered[3], scatter...  26.8 us
    unnamed x193, local copies, waits for them, and re-layouts  26.1 us
    all_to_all x2, starting transfers between devices, return_rows(): lax.all_to_all(buffer, ('grp', 'dev'), split_axis=0, concat_axis=0, tiled...  25.9 us
    dot_general x6, matrix products, spread_rows(): lax.dot_general(onehot, values, (((0,), (0,)), ((), ())), precision=lax.P...  25 us
  transfers between devices with their start and end apart: 7, of which 3 were waited for; matrix products, arithmetic and copies ran while one was open for 13% of the time, Pallas kernels for 0%

commit v1 on v0

v1 whole, which is shorter than its diff:
```python
import functools

import jax
import jax.numpy as jnp
from jax import lax
from jax.experimental import pallas as pl
from jax.experimental.pallas import tpu as pltpu
from jax.sharding import PartitionSpec as P

MESH = pl.DeviceIdType.MESH
BF = jnp.bfloat16
F32 = jnp.float32
H = 4
LOWEST = -1e30
C0 = 0.7978845608028654
C1 = 0.044715


def dot(a, b):
    return jnp.dot(a, b, preferred_element_type=F32)


def dot_nt(a, b):
    return lax.dot_general(a, b, (((1,), (1,)), ((), ())), preferred_element_type=F32)


def dot_tn(a, b):
    return lax.dot_general(a, b, (((0,), (0,)), ((), ())), preferred_element_type=F32)


def iota(shape, axis, kind=jnp.int32):
    return lax.broadcasted_iota(kind, shape, axis)


def gelu_pair(z):
    zz = z * z
    t = jnp.tanh(z * (C0 + (C0 * C1) * zz))
    half = 0.5 * z
    g = half + half * t
    gp = (0.5 + 0.5 * t) + (half - half * (t * t)) * (C0 + (3.0 * C0 * C1) * zz)
    return g, gp


def split(v):
    hi = v.astype(BF)
    return hi, (v - hi.astype(F32)).astype(BF)


def kernel(
    cfg,
    cnt_ref, esrc_ref, etgt_ref, att_ref, bias_ref, gain_ref, shift_ref,
    x_hbm, cot_hbm, ws_hbm, wt_hbm, wr_hbm,
    out_hbm, gf_hbm, small_ref,
    x_v, xt_v, cot_v, fs, fr, rs, rr, wsend, wall, wcat,
    tcolf, trow, srow, th, tht,
    se_v, g_v, ga_v, sc_v, pv_v, sp_v, tp_v, rp_v, sg_v, sga_v, ssc_v, mtab, mx_v,
    dtab, loc_v, a2, eblk, exp2, spread, sel, vecs, vacc, gacc,
    g0s, g0r, g1s, g1r, g2s, g2r,
    in_sem, fs_sem, fr_sem, rs_sem, rr_sem, w_sem, r_sem, out_sem,
):
    NG, ND, X, Y, Z, N, CAP, MB, EC = cfg
    C = 256
    DEV = NG * ND
    E = DEV * CAP
    NCH = E // EC
    PER = EC // CAP
    RW = C // ND
    PK = 3 * RW + 16
    HALF = PK // 2
    NB = min(256, N)
    W8 = 2 * X
    g, d = lax.axis_index("grp"), lax.axis_index("dev")
    mx, mc = lax.div(g, 2), lax.rem(g, 2)
    my, mz = lax.div(d, Z), lax.rem(d, Z)
    twin = (mx * 2 + 1 - mc, d)

    def place(i, q, sign):
        a, k = q // 2, q % 2
        if isinstance(i, int):
            b, c = i % Y, i // Y
            dy, dz = (a + b) % Y, (a + b + c) % Z
        else:
            b, c = lax.rem(i, Y), lax.div(i, Y)
            dy, dz = lax.rem(a + b, Y), lax.rem(a + b + c, Z)
        if sign > 0:
            px, py, pz = mx + a, my + dy, mz + dz
        else:
            px, py, pz = mx + (X - a), my + (Y - dy), mz + (Z - dz)
        return (
            lax.rem(px, X) * 2 + lax.rem(mc + k, 2),
            lax.rem(py, Y) * Z + lax.rem(pz, Z),
        )

    barrier = pltpu.get_barrier_semaphore()

    def greet(i, q):
        pl.semaphore_signal(barrier, inc=1, device_id=place(i, q, 1), device_id_type=MESH)

    def greet_all(i, carry):
        for q in range(W8):
            greet(i, q)
        return carry

    for q in range(1, W8):
        greet(0, q)
    lax.fori_loop(1, DEV // W8, greet_all, 0)
    loads = [
        pltpu.make_async_copy(x_hbm, x_v, in_sem.at[0]),
        pltpu.make_async_copy(ws_hbm, wsend.at[pl.ds(0, RW)], in_sem.at[1]),
        pltpu.make_async_copy(wt_hbm, wsend.at[pl.ds(RW, RW)], in_sem.at[2]),
        pltpu.make_async_copy(wr_hbm, wsend.at[pl.ds(2 * RW, RW)], in_sem.at[3]),
        pltpu.make_async_copy(cot_hbm, cot_v, in_sem.at[4]),
    ]
    for load in loads:
        load.start()

    rep = (iota((RW, C), 1) % RW == iota((RW, C), 0)).astype(F32).astype(BF)
    here = (iota((8, C), 1) // RW == d)
    rows = [jnp.where(here, dot(jnp.broadcast_to(ref[...], (8, RW)), rep), 0.0)
            for ref in (att_ref, bias_ref, gain_ref, shift_ref)]
    line = iota((8, C), 0)
    placed = jnp.zeros((8, C), F32)
    for slot in range(4):
        placed = jnp.where(line == slot, rows[slot], placed)
    wsend[pl.ds(3 * RW, 16), :] = jnp.concatenate([placed, jnp.zeros((8, C), F32)], axis=0).astype(BF)

    def order(sign):
        j = iota((DEV, DEV), 0)
        k = j & 1
        a = (j >> 1) & (X - 1)
        b = (j // W8) & (Y - 1)
        c = j // (W8 * Y)
        dx, dy, dz = a, (a + b) & (Y - 1), (a + b + c) & (Z - 1)
        px = (mx + X + sign * dx) & (X - 1)
        py = (my + Y + sign * dy) & (Y - 1)
        pz = (mz + Z + sign * dz) & (Z - 1)
        dev = (px * 2 + ((mc + k) & 1)) * ND + py * Z + pz
        return (dev == iota((DEV, DEV), 1)).astype(F32).astype(BF)

    TC = min(E, 256)
    LB = 2 * CAP
    lists = []
    for sign, tabs in ((1, esrc_ref), (-1, etgt_ref)):
        perm = order(sign)
        for mb in range(MB):
            parts = jnp.concatenate([tabs[mb, 0] >> 5, tabs[mb, 0] & 31], axis=0)
            lists.append(dot_nt(perm, parts.astype(F32).astype(BF)))
    packed = jnp.concatenate(lists, axis=1).astype(BF)
    LW = 2 * MB * LB
    lane = iota((LW, 2 * MB * 128), 0)
    scale = jnp.where((lane & (LB - 1)) < CAP, 32.0, 1.0)
    widen = jnp.where((lane // LB) == (iota((LW, 2 * MB * 128), 1) // 128), scale, 0.0).astype(BF)
    lane = iota((2 * MB * 16, LW), 1)
    scale = jnp.where((lane & (LB - 1)) < CAP, 32.0, 1.0)
    turn = jnp.where((lane // LB) == (iota((2 * MB * 16, LW), 0) // 16), scale, 0.0).astype(BF)

    def onehot_rows(col):
        wide = jnp.concatenate([col] * (N // 128), axis=1)
        return jnp.where(wide == iota(wide.shape, 1, jnp.int16), jnp.ones((), BF), jnp.zeros((), BF))

    def list_step(i, carry):
        r = pl.multiple_of(i * TC, TC)
        e = iota((TC, DEV), 0) + r
        pairs = ((e // CAP) == iota((TC, DEV), 1)).astype(F32).astype(BF)
        own = (iota((TC, LW), 0) & (CAP - 1)) == (iota((TC, LW), 1) & (CAP - 1))
        kept = jnp.where(own, dot(pairs, packed), 0.0).astype(BF)
        wide = dot(kept, widen)
        flat = dot_nt(turn, kept).astype(jnp.int32).astype(jnp.int16)
        for mb in range(MB):
            out = wide[:, mb * 128:(mb + 1) * 128].astype(jnp.int32).astype(jnp.int16)
            fs[mb, pl.ds(r, TC), :] = dot(onehot_rows(out), x_v[mb]).astype(BF)
            part = wide[:, (MB + mb) * 128:(MB + mb + 1) * 128]
            tcolf[mb, pl.ds(r, TC), :] = part
            th[mb, pl.ds(r, TC), :] = onehot_rows(part.astype(jnp.int32).astype(jnp.int16))
            srow[mb, i] = flat[mb * 16:(mb + 1) * 16, :]
            trow[mb, i] = flat[(MB + mb) * 16:(MB + mb + 1) * 16, :]
        return carry

    loads[0].wait()
    lax.fori_loop(0, E // TC, list_step, 0)

    def fill_turned(row, mb, dst):
        def step(i, carry):
            r = pl.multiple_of(i * 128, 128)
            ids = iota((128, TC), 0, jnp.int16) + (i * 128).astype(jnp.int16)
            for q in range(E // TC):
                wide = jnp.concatenate([row[mb, q]] * 8, axis=0)
                dst[mb, pl.ds(r, 128), q * TC:(q + 1) * TC] = jnp.where(
                    wide == ids, jnp.ones((), BF), jnp.zeros((), BF)
                )
            return carry

        lax.fori_loop(0, N // 128, step, 0)

    for mb in range(MB):
        fill_turned(trow, mb, tht)
    for load in loads[1:4]:
        load.wait()

    pl.semaphore_wait(barrier, DEV - 1)

    half = pl.ds(pl.multiple_of(mc * HALF, 16), HALF)

    def send_weights(i, carry):
        pltpu.make_async_remote_copy(
            src_ref=wsend.at[half], dst_ref=wall.at[d, half],
            send_sem=w_sem.at[0], recv_sem=w_sem.at[1],
            device_id=(g, lax.rem(d + i, ND)), device_id_type=MESH,
        ).start()
        return carry

    lax.fori_loop(1, ND, send_weights, 0)
    pltpu.make_async_copy(wsend.at[half], wall.at[d, half], w_sem.at[1]).start()

    def send_block(src, dst, mb, i, q, sign, ssem, rsem):
        rows = pl.ds(pl.multiple_of((i * W8 + q) * CAP, CAP), CAP)
        chunk = i * W8 // PER if isinstance(i, int) else lax.div(i, PER // W8)
        pltpu.make_async_remote_copy(
            src_ref=src.at[mb, rows], dst_ref=dst.at[mb, rows],
            send_sem=ssem.at[mb], recv_sem=rsem.at[mb, chunk],
            device_id=place(i, q, sign), device_id_type=MESH,
        ).start()

    def keep_block(src, dst, mb, rsem):
        pltpu.make_async_copy(
            src.at[mb, pl.ds(0, CAP)], dst.at[mb, pl.ds(0, CAP)], rsem.at[mb, 0]
        ).start()

    def send_rows(mb, carry):
        keep_block(fs, fr, mb, fr_sem)
        for q in range(1, W8):
            send_block(fs, fr, mb, 0, q, 1, fs_sem, fr_sem)

        def more(i, carry):
            for q in range(W8):
                send_block(fs, fr, mb, i, q, 1, fs_sem, fr_sem)
            return carry

        lax.fori_loop(1, DEV // W8, more, 0)
        return carry

    lax.fori_loop(0, MB, send_rows, 0)

    for mb in range(MB):
        for i in range(N // 128):
            xt_v[mb, :, i * 128:(i + 1) * 128] = jnp.transpose(x_v[mb, i * 128:(i + 1) * 128, :])

    same = (iota((C, C), 0) // 64) == (iota((C, C), 1) // 64)
    eblk[...] = same.astype(F32).astype(BF)
    lane = iota((128, C), 0)
    head = iota((128, C), 1) // 64
    exp2[...] = ((lane < 8) & ((lane & 3) == head)).astype(F32).astype(BF)
    groups = N // 64
    r = lane & 63
    at = 2 * ((r & 31) // groups) + r // 32
    spread[...] = ((at == head) & ((r & 31) < 2 * groups)).astype(F32).astype(BF)
    pick = iota((C, 128), 0)
    slot = iota((C, 128), 1)
    sel[0] = ((pick == 64 * slot) & (slot < 4)).astype(F32).astype(BF)
    sel[1] = ((pick == 64 * (slot - 4)) & (slot >= 4) & (slot < 8)).astype(F32).astype(BF)
    vacc[...] = jnp.zeros_like(vacc)
    gacc[...] = jnp.zeros_like(gacc)

    mine = wall.at[:, half]
    pltpu.make_async_copy(mine, mine, w_sem.at[1]).wait()
    pltpu.make_async_remote_copy(
        src_ref=mine, dst_ref=mine, send_sem=w_sem.at[2], recv_sem=w_sem.at[3],
        device_id=twin, device_id_type=MESH,
    ).start()
    pltpu.make_async_copy(mine, mine, w_sem.at[3]).wait()
    for slot in range(3):
        wcat[:, slot * C:(slot + 1) * C] = wall[:, slot * RW:(slot + 1) * RW, :].reshape(C, C)
    vectors = jnp.sum(wall[:, 3 * RW:3 * RW + 16, :].astype(F32), axis=0)
    vecs[...] = vectors[0:8, :]
    att_col = jnp.transpose(jnp.broadcast_to(vecs[0:1, :], (C, C)))
    a2[...] = jnp.where(same, att_col, 0.0).astype(BF)

    def project(i, carry):
        mb, part = lax.div(i, N // NB), lax.rem(i, N // NB)
        rows = pl.ds(pl.multiple_of(part * NB, NB), NB)
        proj = dot(x_v[mb, rows, :], wcat[...])
        sp = proj[:, 0:C].astype(BF)
        tp = proj[:, C:2 * C]
        sp_v[mb, rows, :] = sp
        tp_v[mb, rows, :] = tp.astype(BF)
        rp_v[mb, rows, :] = proj[:, 2 * C:3 * C]
        gs, gp = gelu_pair(sp.astype(F32) + tp)
        hi, lo = split(gs)
        sg_v[mb, rows, :] = hi
        sga_v[mb, rows, :] = gp * vecs[0:1, :]
        ssc_v[mb, rows, :] = dot(hi, a2[...]) + dot(lo, a2[...])
        return carry

    lax.fori_loop(0, MB * (N // NB), project, 0)
    loads[4].wait()

    def fold(v):
        return jnp.sum(v.reshape(v.shape[0] // 8, 8, v.shape[1]), axis=0)

    def edge_rows(i):
        return slice(i * EC, (i + 1) * EC)

    def score_chunk(mb, i):
        rows = edge_rows(i)
        part = fr.at[mb, pl.ds(i * EC, EC)]
        pltpu.make_async_copy(part, part, fr_sem.at[mb, i]).wait()
        se = dot(fr[mb, rows, :], wcat[:, 0:C]).astype(BF)
        se_v[rows, :] = se
        z = se.astype(F32) + dot(th[mb, rows, :], tp_v[mb])
        ge, gp = gelu_pair(z)
        hi, lo = split(ge)
        g_v[rows, :] = hi
        ga_v[rows, :] = gp * vecs[0:1, :]
        sc_v[rows, :] = dot(hi, a2[...]) + dot(lo, a2[...])

    def sweep_chunk(mb, i):
        low = (iota((128, 128), 1) & 63).astype(F32)
        for q in range(EC // 128):
            part = slice(i * EC + q * 128, i * EC + (q + 1) * 128)
            tgt = tcolf[mb, part, :]
            s0, s1 = sc_v[part, 0:128], sc_v[part, 128:256]
            for grp in range(groups):
                hit = tgt == low + (64.0 * grp)
                for side, s in enumerate((s0, s1)):
                    top = jnp.max(jnp.where(hit, s, LOWEST).reshape(16, 8, 128), axis=0)
                    at = side * groups + grp
                    mx_v[at] = jnp.maximum(mx_v[at], top)

    def forward_edges(mb):
        mx_v[...] = jnp.full(mx_v.shape, LOWEST, F32)
        for i in range(NCH):
            score_chunk(mb, i)
            if i > 0:
                sweep_chunk(mb, i - 1)
        sweep_chunk(mb, NCH - 1)

    def tops(mb):
        best = jnp.max(mx_v[...], axis=1)
        best = jnp.concatenate([best, jnp.zeros((128 - 2 * groups, 128), F32)], axis=0)
        turned = jnp.transpose(best)
        both = turned[0:64, :] + pltpu.roll(turned[64:128, :], 32, 1)
        hi = both.astype(BF).astype(F32)
        table = hi + pltpu.roll(both - hi, 64, 1)
        for i in range(N // NB):
            rows = slice(i * NB, (i + 1) * NB)
            whose = iota((NB, 128), 0) // 64 + i * (NB // 64)
            mine = jnp.concatenate([table] * (NB // 64), axis=0)
            mine = jnp.where((iota((NB, 128), 1) & (groups - 1)) == whose, mine, 0.0).astype(BF)
            own = ssc_v[mb, rows, :]
            hi, lo = split(jnp.maximum(dot(mine, spread[...]), own))
            ssc_v[mb, rows, :] = jnp.exp(own - (hi.astype(F32) + lo.astype(F32)))
            mtab[rows, :] = (dot(hi, sel[0]) + dot(lo, sel[1])).astype(BF)

    def weigh(mb):
        for i in range(NCH):
            rows = edge_rows(i)
            me = dot(th[mb, rows, :], mtab[...]).astype(BF)
            live = tcolf[mb, rows, :] >= 0.0
            live = jnp.concatenate([live, live], axis=1)
            p = jnp.where(live, jnp.exp(sc_v[rows, :] - dot(me, exp2[...])), 0.0)
            pv_v[rows, 0:C] = (p * se_v[rows, :].astype(F32)).astype(BF)
            pv_v[rows, C:2 * C] = p.astype(BF)

    def nodes(mb):
        for i in range(N // NB):
            rows = slice(i * NB, (i + 1) * NB)
            sc_v[rows, :] = dot(tht[mb, rows, :], pv_v[:, 0:C])
            sc_v[N + i * NB:N + (i + 1) * NB, :] = dot(tht[mb, rows, :], pv_v[:, C:2 * C])
        for i in range(N // NB):
            r = i * NB
            rows = slice(r, r + NB)
            ps = ssc_v[mb, rows, :]
            inv = 1.0 / (sc_v[N + r:N + r + NB, :] + ps)
            sp = sp_v[mb, rows, :].astype(F32)
            agg = (sc_v[rows, :] + ps * sp) * inv
            alpha = ps * inv
            live = (iota((NB, 1), 0) + r < cnt_ref[0, mb]).astype(F32)
            pre = agg + vecs[1:2, :] + rp_v[mb, rows, :]
            centre = pre - jnp.mean(pre, axis=1, keepdims=True)
            rstd = lax.rsqrt(jnp.mean(centre * centre, axis=1, keepdims=True) + 1e-05)
            nrm = centre * rstd
            lin = nrm * vecs[2:3, :] + vecs[3:4, :]
            e = jnp.exp(jnp.minimum(lin, 0.0))
            up = lin > 0
            x_v2 = jnp.where(up, lin, e - 1.0) * live
            cot = cot_v[mb, rows, :].astype(F32) * live
            cot_v[mb, rows, :] = x_v2.astype(BF)
            dlin = cot * jnp.where(up, 1.0, e)
            vacc[2] += fold(dlin * nrm)
            vacc[3] += fold(dlin)
            dn = dlin * vecs[2:3, :]
            dpre = rstd * (
                dn
                - jnp.mean(dn, axis=1, keepdims=True)
                - nrm * jnp.mean(dn * nrm, axis=1, keepdims=True)
            )
            vacc[1] += fold(dpre)
            loc_v[mb, rows, 2 * C:3 * C] = dpre.astype(BF)
            dagr = (dpre * inv).astype(BF)
            dagf = dagr.astype(F32)
            hi, lo = split(dagf * agg)
            big = dot(hi, eblk[...]) + dot(lo, eblk[...])
            hi, lo = split(dagf * (sp - agg))
            ds = ps * (dot(hi, eblk[...]) + dot(lo, eblk[...]))
            vacc[0] += fold(ds * sg_v[mb, rows, :].astype(F32))
            dz = ds * sga_v[mb, rows, :].astype(F32)
            loc_v[mb, rows, C:2 * C] = dz.astype(BF)
            loc_v[mb, rows, 0:C] = (alpha * dpre + dz).astype(BF)
            dtab[rows, 0:C] = dagr
            hi, lo = split(big)
            dtab[rows, C:C + 128] = (dot(hi, sel[0]) + dot(lo, sel[1])).astype(BF)

    def grad_chunk(mb, i):
        rows = edge_rows(i)
        got = dot(th[mb, rows, :], dtab[...])
        dag = got[:, 0:C]
        se = se_v[rows, :].astype(F32)
        hi, lo = split(dag * se)
        p = pv_v[rows, C:2 * C].astype(F32)
        ds = p * (dot(hi, eblk[...]) + dot(lo, eblk[...]) - dot(got[:, C:C + 128].astype(BF), exp2[...]))
        vacc[0] += fold(ds * g_v[rows, :].astype(F32))
        dz = ds * ga_v[rows, :]
        eg = (p * dag + dz).astype(BF)
        rs[mb, rows, :] = eg
        gacc[:, 0:C] += dot_tn(fr[mb, rows, :], eg)
        fr[mb, rows, :] = dz.astype(BF)

    def return_chunk(mb, i):
        if i == 0:
            keep_block(rs, rr, mb, rr_sem)
        for j in range(max(1, i * PER), (i + 1) * PER):
            send_block(rs, rr, mb, j // W8, j % W8, -1, rs_sem, rr_sem)

    def backward_edges(mb):
        for i in range(NCH):
            grad_chunk(mb, i)
            if i > 0:
                return_chunk(mb, i - 1)
        return_chunk(mb, NCH - 1)

    def one_batch(mb, carry):
        forward_edges(mb)
        tops(mb)
        weigh(mb)
        nodes(mb)
        pltpu.make_async_copy(cot_v.at[mb], out_hbm.at[mb], out_sem.at[mb]).start()
        backward_edges(mb)
        return carry

    lax.fori_loop(0, MB, one_batch, 0)

    def local_grads(mb, carry):
        for i in range(N // NB):
            rows = slice(i * NB, (i + 1) * NB)
            dtgt = dot(tht[mb, rows, :], fr[mb]) + loc_v[mb, rows, C:2 * C].astype(F32)
            loc_v[mb, rows, C:2 * C] = dtgt.astype(BF)
        gacc[...] += dot(xt_v[mb], loc_v[mb])
        return carry

    lax.fori_loop(0, MB, local_grads, 0)

    def pack_vectors(v):
        hi = v.astype(BF).astype(F32)
        return jnp.concatenate([hi, v - hi], axis=0).astype(BF)

    def repack(v):
        cut = HALF - 16
        both = v[..., cut:cut + 8, :] + v[..., cut + 8:cut + 16, :]
        hi = both.astype(BF).astype(F32)
        last = jnp.concatenate([hi, both - hi], axis=-2)
        last = jnp.where(mc == 1, last, v[..., cut:cut + 16, :])
        return jnp.concatenate([v[..., 0:cut, :], last], axis=-2).astype(BF)

    for slot in range(3):
        g0s[:, slot * RW:(slot + 1) * RW, :] = gacc[:, slot * C:(slot + 1) * C].astype(BF).reshape(ND, RW, C)
    sums = [jnp.sum(vacc[slot], axis=0, keepdims=True) for slot in range(4)]
    packed = pack_vectors(jnp.concatenate(sums + [jnp.zeros((4, C), F32)], axis=0))
    for slot in range(ND):
        g0s[slot, 3 * RW:3 * RW + 16, :] = packed
    other = pl.ds(pl.multiple_of((1 - mc) * HALF, 16), HALF)
    pltpu.make_async_remote_copy(
        src_ref=g0s.at[:, other], dst_ref=g0r, send_sem=r_sem.at[4], recv_sem=r_sem.at[5],
        device_id=twin, device_id_type=MESH,
    ).start()

    def partials(mb, carry):
        for i in range(N // NB):
            rows = slice(i * NB, (i + 1) * NB)
            rp_v[mb, rows, :] = dot_nt(loc_v[mb, rows, C:3 * C], wcat[:, C:3 * C])
        fill_turned(srow, mb, tht)
        return carry

    partials(0, 0)
    pltpu.make_async_copy(g0r, g0r, r_sem.at[5]).wait()
    g1s[...] = repack(g0s[:, half, :].astype(F32) + g0r[...].astype(F32))

    def send_first(i, carry):
        to = lax.rem(d + i, ND)
        pltpu.make_async_remote_copy(
            src_ref=g1s.at[to], dst_ref=g1r.at[d], send_sem=r_sem.at[0], recv_sem=r_sem.at[1],
            device_id=(g, to), device_id_type=MESH,
        ).start()
        return carry

    lax.fori_loop(1, ND, send_first, 0)
    pltpu.make_async_copy(g1s.at[d], g1r.at[d], r_sem.at[1]).start()
    partials(1, 0)

    def finish(mb):
        for i in range(NCH):
            rows = pl.ds(i * EC, EC)
            pltpu.make_async_copy(rr.at[mb, rows], rr.at[mb, rows], rr_sem.at[mb, i]).wait()
        pltpu.make_async_copy(cot_v.at[mb], out_hbm.at[mb], out_sem.at[mb]).wait()

        def step(i, carry):
            rows = pl.ds(pl.multiple_of(i * NB, NB), NB)
            dsrc = (dot(tht[mb, rows, :], rr[mb]) + loc_v[mb, rows, 0:C].astype(F32)).astype(BF)
            cot_v[mb, rows, :] = (dot_nt(dsrc, wcat[:, 0:C]) + rp_v[mb, rows, :]).astype(BF)
            return carry

        lax.fori_loop(0, N // NB, step, 0)
        pltpu.make_async_copy(cot_v.at[mb], gf_hbm.at[mb], out_sem.at[mb]).start()

    finish(0)

    pltpu.make_async_copy(g1r, g1r, r_sem.at[1]).wait()
    g2s[...] = repack(jnp.sum(g1r[...].astype(F32), axis=0))

    def send_second(i, carry):
        pltpu.make_async_remote_copy(
            src_ref=g2s, dst_ref=g2r.at[g], send_sem=r_sem.at[2], recv_sem=r_sem.at[3],
            device_id=(lax.rem(g + i, NG), d), device_id_type=MESH,
        ).start()
        return carry

    lax.fori_loop(1, NG, send_second, 0)
    pltpu.make_async_copy(g2s, g2r.at[g], r_sem.at[3]).start()

    for mb in range(1, MB):
        finish(mb)

    pltpu.make_async_copy(g2r, g2r, r_sem.at[3]).wait()
    for side in range(2):
        total = g2r[side].astype(F32)
        for slot in range(1, X):
            total = total + g2r[2 * slot + side].astype(F32)
        small_ref[side * HALF:(side + 1) * HALF, :] = total
    tail = small_ref[3 * RW:3 * RW + 8, :] + small_ref[3 * RW + 8:3 * RW + 16, :]
    small_ref[3 * RW:3 * RW + 8, :] = pltpu.roll(tail, lax.rem(C - d * RW, C), 1)

    for mb in range(MB):
        pltpu.make_async_copy(cot_v.at[mb], gf_hbm.at[mb], out_sem.at[mb]).wait()
        most = pl.ds(0, (DEV - 1) * CAP)
        pltpu.make_async_copy(fs.at[mb, most], fs.at[mb, most], fs_sem.at[mb]).wait()
        pltpu.make_async_copy(rs.at[mb, most], rs.at[mb, most], rs_sem.at[mb]).wait()
    pltpu.make_async_copy(mine, mine, w_sem.at[2]).wait()
    others = pl.ds(0, ND - 1)
    mine = wall.at[others, half]
    pltpu.make_async_copy(mine, mine, w_sem.at[0]).wait()
    pltpu.make_async_copy(g0r, g0r, r_sem.at[4]).wait()
    pltpu.make_async_copy(g1s.at[others], g1s.at[others], r_sem.at[0]).wait()
    others = pl.ds(0, NG - 1)
    pltpu.make_async_copy(g2r.at[others], g2r.at[others], r_sem.at[2]).wait()


def hand_on(RW, out_in, gf_in, small_in, out_hbm, gf_hbm, gws, gwt, gwr, v0, v1, v2, v3, held, sems):
    MB = out_in.shape[0]
    loads, stores = [], []
    for mb in range(MB):
        for src, dst in ((out_in, out_hbm), (gf_in, gf_hbm)):
            slot = len(loads)
            loads.append(pltpu.make_async_copy(src.at[mb], held.at[slot], sems.at[0, slot]))
            stores.append(pltpu.make_async_copy(held.at[slot], dst.at[mb], sems.at[1, slot]))
    for load in loads:
        load.start()
    for slot, dst in enumerate((gws, gwt, gwr)):
        dst[...] = small_in[slot * RW:(slot + 1) * RW, :]
    for slot, dst in enumerate((v0, v1, v2, v3)):
        dst[...] = small_in[3 * RW + slot:3 * RW + slot + 1, 0:RW]
    for load, store in zip(loads, stores):
        load.wait()
        store.start()
    for store in stores:
        store.wait()


def local(
    shape,
    features, w_source, w_target, w_residual, attention, out_bias, norm_gain, norm_shift,
    node_count, edge_src, edge_tgt, cotangent,
):
    NG, ND = shape
    X = NG // 2
    Y = 1
    while Y * Y < ND:
        Y *= 2
    Z = ND // Y
    MB, N, C = features.shape
    CAP = edge_src.shape[3]
    DEV = NG * ND
    E = DEV * CAP
    EC = min(256, E // 2)
    NCH = E // EC
    RW = C // ND
    PK = 3 * RW + 16
    groups = N // 64
    TC = min(E, 256)
    vmem = pl.BlockSpec(memory_space=pltpu.VMEM)
    hbm = pl.BlockSpec(memory_space=pl.ANY)
    smem = pl.BlockSpec(memory_space=pltpu.SMEM)
    cfg = (NG, ND, X, Y, Z, N, CAP, MB, EC)
    V = pltpu.VMEM
    DMA = pltpu.SemaphoreType.DMA
    I16 = jnp.int16
    wide = jax.ShapeDtypeStruct((MB, N, C), BF)
    block = jax.ShapeDtypeStruct((RW, C), F32)
    line = jax.ShapeDtypeStruct((1, RW), F32)
    result, grad_rows, small = pl.pallas_call(
        functools.partial(kernel, cfg),
        out_shape=(wide, wide, jax.ShapeDtypeStruct((PK, C), F32)),
        in_specs=[smem] + [vmem] * 6 + [hbm] * 5,
        out_specs=(hbm, hbm, vmem),
        scratch_shapes=[
            V((MB, N, C), BF), V((MB, C, N), BF), V((MB, N, C), BF),
            V((MB, E, C), BF), V((MB, E, C), BF), V((MB, E, C), BF), V((MB, E, C), BF),
            V((PK, C), BF), V((ND, PK, C), BF), V((C, 3 * C), BF),
            V((MB, E, 128), F32),
            V((MB, E // TC, 16, TC), I16), V((MB, E // TC, 16, TC), I16),
            V((MB, E, N), BF), V((MB, N, E), BF),
            V((E, C), BF), V((E, C), BF), V((E, C), F32), V((max(E, 2 * N), C), F32), V((E, 2 * C), BF),
            V((MB, N, C), BF), V((MB, N, C), BF), V((MB, N, C), F32),
            V((MB, N, C), BF), V((MB, N, C), F32), V((MB, N, C), F32),
            V((N, 128), BF), V((2 * groups, 8, 128), F32),
            V((N, C + 128), BF), V((MB, N, 3 * C), BF),
            V((C, C), BF), V((C, C), BF), V((128, C), BF), V((128, C), BF), V((2, C, 128), BF),
            V((8, C), F32), V((4, 8, C), F32), V((C, 3 * C), F32),
            V((ND, PK, C), BF), V((ND, PK // 2, C), BF), V((ND, PK // 2, C), BF),
            V((ND, PK // 2, C), BF), V((PK // 2, C), BF), V((NG, PK // 2, C), BF),
            DMA((5,)), DMA((MB,)), DMA((MB, NCH)), DMA((MB,)), DMA((MB, NCH)),
            DMA((4,)), DMA((6,)), DMA((MB,)),
        ],
        compiler_params=pltpu.CompilerParams(
            collective_id=0, has_side_effects=True, vmem_limit_bytes=62 * 2**20
        ),
        cost_estimate=pl.CostEstimate(
            flops=20 * MB * E * N * C, bytes_accessed=10 * MB * N * C, transcendentals=4 * MB * E * C
        ),
    )(
        jnp.swapaxes(node_count, 0, 1), jnp.swapaxes(edge_src, 2, 3), jnp.swapaxes(edge_tgt, 2, 3),
        attention.reshape(1, RW), out_bias.reshape(1, RW), norm_gain.reshape(1, RW), norm_shift.reshape(1, RW),
        features, cotangent, w_source, w_target, w_residual,
    )
    outs = pl.pallas_call(
        functools.partial(hand_on, RW),
        out_shape=(wide, wide, block, block, block, line, line, line, line),
        in_specs=[hbm, hbm, vmem],
        out_specs=(hbm, hbm) + (vmem,) * 7,
        scratch_shapes=[V((2 * MB, N, C), BF), DMA((2, 2 * MB))],
    )(result, grad_rows, small)
    return outs[:5] + tuple(v.reshape(RW) for v in outs[5:])


def solution(mesh):
    shape = (mesh.shape["grp"], mesh.shape["dev"])
    return jax.shard_map(
        functools.partial(local, shape),
        mesh=mesh,
        in_specs=(
            P(None, ("grp", "dev"), None),
            P("dev", None),
            P("dev", None),
            P("dev", None),
            P("dev"),
            P("dev"),
            P("dev"),
            P("dev"),
            P(None, ("grp", "dev")),
            P(None, ("grp", "dev"), None, None),
            P(None, ("grp", "dev"), None, None),
            P(None, ("grp", "dev"), None),
        ),
        out_specs=(
            P(None, ("grp", "dev"), None),
            P(None, ("grp", "dev"), None),
            P("dev", None),
            P("dev", None),
            P("dev", None),
            P("dev"),
            P("dev"),
            P("dev"),
            P("dev"),
        ),
        check_vma=False,
    )
```

time: 637 us -> 109 us (0.17); the launches traced: 626 us -> 109 us
  blocking collectives: 156 us -> 0 us
  waiting for transfers between devices: 153 us -> 0 us
  Pallas kernels: 0 us -> 108 us
  matrix products: 89.5 us -> 0 us
  local copies, waits for them, and re-layouts: 84.4 us -> 0 us
  other arithmetic: 67.7 us -> 0 us
  starting transfers between devices: 59.3 us -> 0 us
  between operations: 16.4 us -> 0.84 us
    unnamed x6 -> x0, waiting for transfers between devices: 153 us -> none
    pallas_call x0 -> x2, Pallas kernels: none -> 108 us  [the longest x1 104 us: local(): pl.pallas_call(functools.partial(kernel, cfg), out_shape=(wide, wide, jax...]
    dot_general x38 -> x0, matrix products: 89.5 us -> none  [the longest x10 34.1 us: pick_rows(): jnp.dot(onehot, table, precision=lax.Precision.HIGH, preferred_element_ty...]
    unnamed x2 -> x0, blocking collectives: 69.6 us -> none
    all_gather x3 -> x0, blocking collectives: 59.9 us -> none  [the longest x1 23.8 us: local(): lax.all_gather(w_residual, 'dev', axis=0, tiled=True)]
    all_to_all x4 -> x0, starting transfers between devices: 58.8 us -> none  [the longest x2 32.9 us: send_rows(): lax.all_to_all(buffer, ('grp', 'dev'), split_axis=0, concat_axis=0, tiled...]
    reduce_sum x13 -> x0, other arithmetic: 33.4 us -> none  [the longest x2 11 us: one_batch(): jnp.sum(edge_dscore[:, :, None] * edge_unit, axis=0)]
    psum x1 -> x0, blocking collectives: 26.8 us -> none  [local(): lax.psum((scattered[0], scattered[1], scattered[2], scattered[3], scatter...]
  transfers between devices with their start and end apart: 7 -> 0, of which waited for: 3 -> 0; matrix products, arithmetic and copies ran while one was open for 13% -> 0% of each run, Pallas kernels for 0% -> 0%
where the time goes in v1:
time: 109 us
  Pallas kernels  108 us (99%)
    pallas_call x1, Pallas kernels, local(): pl.pallas_call(functools.partial(kernel, cfg), out_shape=(wide, wide, jax...  104 us
    pallas_call x1, Pallas kernels, local(): pl.pallas_call(functools.partial(hand_on, RW), out_shape=(wide, wide, blo...  3.89 us

profile of v1, /device:TPU:1, one launch (start us, length us, event | category | flops | bytes accessed | tf_op | source)
XLA Modules:
  0.0 108.7 jit_solution(7729359346259933776)
XLA Ops:
  0.6 104.0 %shard_map.187 = (bf16[2,1024,256]{2,1,0:T(8,128)(2,1)}, bf16[2,1024,256]{2,1,0:T(8,128)(2,1)}, f32[64,256]{1,0:T(8,128)}) custom-call(s32[1,2]{1,0:T(1,128)} %bitcast.13, s32[2,1,16,128]{3,2,1,0:T(8,128)} %bitcast.11, s32[2,1,16,128]{3,2,1,0:T(8,128)} %bitcast.12, bf16[1,16]{1,0:T(2,128)(2,1)} %bitcast.14, bf16[1,16]{1,0:T(2,128)(2,1)} %bitcast.15, ...), custom_call_target="tpu_custom_call" | custom-call | flops 21474836480 | bytes 5242880 | tf_op jit(solution)/shard_map/pallas_call | solution.py:618
  104.6 3.9 %shard_map.188 = (bf16[2,1024,256]{2,1,0:T(8,128)(2,1)}, bf16[2,1024,256]{2,1,0:T(8,128)(2,1)}, f32[16,256]{1,0:T(8,128)}, f32[16,256]{1,0:T(8,128)}, f32[16,256...) custom-call(bf16[2,1024,256]{2,1,0:T(8,128)(2,1)} %get-tuple-element.21.out_in, ...), custom_call_target="tpu_custom_call" | custom-call | tf_op jit(solution)/shard_map/pallas_call | solution.py:653

commit v2 on v1

--- a/solution.py
+++ b/solution.py
@@ -52,7 +52,7 @@
     x_hbm, cot_hbm, ws_hbm, wt_hbm, wr_hbm,
     out_hbm, gf_hbm, small_ref,
     x_v, xt_v, cot_v, fs, fr, rs, rr, wsend, wall, wcat,
-    tcolf, trow, srow, th, tht,
+    lists, tcolf, trow, srow, th, tht,
     se_v, g_v, ga_v, sc_v, pv_v, sp_v, tp_v, rp_v, sg_v, sga_v, ssc_v, mtab, mx_v,
     dtab, loc_v, a2, eblk, exp2, spread, sel, vecs, vacc, gacc,
     g0s, g0r, g1s, g1r, g2s, g2r,
@@ -137,68 +137,72 @@
         dev = (px * 2 + ((mc + k) & 1)) * ND + py * Z + pz
         return (dev == iota((DEV, DEV), 1)).astype(F32).astype(BF)
 
-    TC = min(E, 256)
     LB = 2 * CAP
-    lists = []
-    for sign, tabs in ((1, esrc_ref), (-1, etgt_ref)):
-        perm = order(sign)
-        for mb in range(MB):
-            parts = jnp.concatenate([tabs[mb, 0] >> 5, tabs[mb, 0] & 31], axis=0)
-            lists.append(dot_nt(perm, parts.astype(F32).astype(BF)))
-    packed = jnp.concatenate(lists, axis=1).astype(BF)
-    LW = 2 * MB * LB
-    lane = iota((LW, 2 * MB * 128), 0)
-    scale = jnp.where((lane & (LB - 1)) < CAP, 32.0, 1.0)
-    widen = jnp.where((lane // LB) == (iota((LW, 2 * MB * 128), 1) // 128), scale, 0.0).astype(BF)
-    lane = iota((2 * MB * 16, LW), 1)
-    scale = jnp.where((lane & (LB - 1)) < CAP, 32.0, 1.0)
-    turn = jnp.where((lane // LB) == (iota((2 * MB * 16, LW), 0) // 16), scale, 0.0).astype(BF)
+
+    def list_of(slot, sign, tabs, mb):
+        parts = jnp.concatenate([tabs[mb, 0] >> 5, tabs[mb, 0] & 31], axis=0)
+        lists[slot] = dot_nt(order(sign), parts.astype(F32).astype(BF)).astype(BF)
+
+    def expand(slot, i):
+        e = iota((EC, DEV), 0) + i * EC
+        pairs = ((e // CAP) == iota((EC, DEV), 1)).astype(F32).astype(BF)
+        own = (iota((EC, LB), 0) & (CAP - 1)) == (iota((EC, LB), 1) & (CAP - 1))
+        kept = jnp.where(own, dot(pairs, lists[slot]), 0.0).astype(BF)
+        widen = jnp.where(iota((LB, 128), 0) < CAP, 32.0, 1.0).astype(BF)
+        turn = jnp.where(iota((16, LB), 1) < CAP, 32.0, 1.0).astype(BF)
+        return dot(kept, widen), dot_nt(turn, kept).astype(jnp.int32).astype(jnp.int16)
 
     def onehot_rows(col):
         wide = jnp.concatenate([col] * (N // 128), axis=1)
         return jnp.where(wide == iota(wide.shape, 1, jnp.int16), jnp.ones((), BF), jnp.zeros((), BF))
 
-    def list_step(i, carry):
-        r = pl.multiple_of(i * TC, TC)
-        e = iota((TC, DEV), 0) + r
-        pairs = ((e // CAP) == iota((TC, DEV), 1)).astype(F32).astype(BF)
-        own = (iota((TC, LW), 0) & (CAP - 1)) == (iota((TC, LW), 1) & (CAP - 1))
-        kept = jnp.where(own, dot(pairs, packed), 0.0).astype(BF)
-        wide = dot(kept, widen)
-        flat = dot_nt(turn, kept).astype(jnp.int32).astype(jnp.int16)
-        for mb in range(MB):
-            out = wide[:, mb * 128:(mb + 1) * 128].astype(jnp.int32).astype(jnp.int16)
-            fs[mb, pl.ds(r, TC), :] = dot(onehot_rows(out), x_v[mb]).astype(BF)
-            part = wide[:, (MB + mb) * 128:(MB + mb + 1) * 128]
-            tcolf[mb, pl.ds(r, TC), :] = part
-            th[mb, pl.ds(r, TC), :] = onehot_rows(part.astype(jnp.int32).astype(jnp.int16))
-            srow[mb, i] = flat[mb * 16:(mb + 1) * 16, :]
-            trow[mb, i] = flat[(MB + mb) * 16:(MB + mb + 1) * 16, :]
-        return carry
-
-    loads[0].wait()
-    lax.fori_loop(0, E // TC, list_step, 0)
-
     def fill_turned(row, mb, dst):
         def step(i, carry):
             r = pl.multiple_of(i * 128, 128)
-            ids = iota((128, TC), 0, jnp.int16) + (i * 128).astype(jnp.int16)
-            for q in range(E // TC):
+            ids = iota((128, EC), 0, jnp.int16) + (i * 128).astype(jnp.int16)
+            for q in range(NCH):
                 wide = jnp.concatenate([row[mb, q]] * 8, axis=0)
-                dst[mb, pl.ds(r, 128), q * TC:(q + 1) * TC] = jnp.where(
+                dst[mb, pl.ds(r, 128), q * EC:(q + 1) * EC] = jnp.where(
                     wide == ids, jnp.ones((), BF), jnp.zeros((), BF)
                 )
             return carry
 
         lax.fori_loop(0, N // 128, step, 0)
 
+    def send_block(src, dst, mb, j, sign, ssem, rsem):
+        rows = pl.ds(j * CAP, CAP)
+        pltpu.make_async_remote_copy(
+            src_ref=src.at[mb, rows], dst_ref=dst.at[mb, rows],
+            send_sem=ssem.at[mb], recv_sem=rsem.at[mb, j // PER],
+            device_id=place(j // W8, j % W8, sign), device_id_type=MESH,
+        ).start()
+
+    def send_chunk(src, dst, mb, i, sign, ssem, rsem):
+        if i == 0:
+            pltpu.make_async_copy(
+                src.at[mb, pl.ds(0, CAP)], dst.at[mb, pl.ds(0, CAP)], rsem.at[mb, 0]
+            ).start()
+        for j in range(max(1, i * PER), (i + 1) * PER):
+            send_block(src, dst, mb, j, sign, ssem, rsem)
+
     for mb in range(MB):
-        fill_turned(trow, mb, tht)
+        list_of(mb, 1, esrc_ref, mb)
+    loads[0].wait()
+    pl.semaphore_wait(barrier, DEV - 1)
+
+    def outgoing(mb, carry):
+        for i in range(NCH):
+            wide, flat = expand(mb, i)
+            srow[mb, i] = flat
+            hot = onehot_rows(wide.astype(jnp.int32).astype(jnp.int16))
+            fs[mb, i * EC:(i + 1) * EC, :] = dot(hot, x_v[mb]).astype(BF)
+            if i > 0:
+                send_chunk(fs, fr, mb, i - 1, 1, fs_sem, fr_sem)
+        send_chunk(fs, fr, mb, NCH - 1, 1, fs_sem, fr_sem)
+        return carry
+
     for load in loads[1:4]:
         load.wait()
-
-    pl.semaphore_wait(barrier, DEV - 1)
-
     half = pl.ds(pl.multiple_of(mc * HALF, 16), HALF)
 
     def send_weights(i, carry):
@@ -212,35 +216,22 @@
     lax.fori_loop(1, ND, send_weights, 0)
     pltpu.make_async_copy(wsend.at[half], wall.at[d, half], w_sem.at[1]).start()
 
-    def send_block(src, dst, mb, i, q, sign, ssem, rsem):
-        rows = pl.ds(pl.multiple_of((i * W8 + q) * CAP, CAP), CAP)
-        chunk = i * W8 // PER if isinstance(i, int) else lax.div(i, PER // W8)
-        pltpu.make_async_remote_copy(
-            src_ref=src.at[mb, rows], dst_ref=dst.at[mb, rows],
-            send_sem=ssem.at[mb], recv_sem=rsem.at[mb, chunk],
-            device_id=place(i, q, sign), device_id_type=MESH,
-        ).start()
-
-    def keep_block(src, dst, mb, rsem):
-        pltpu.make_async_copy(
-            src.at[mb, pl.ds(0, CAP)], dst.at[mb, pl.ds(0, CAP)], rsem.at[mb, 0]
-        ).start()
-
-    def send_rows(mb, carry):
-        keep_block(fs, fr, mb, fr_sem)
-        for q in range(1, W8):
-            send_block(fs, fr, mb, 0, q, 1, fs_sem, fr_sem)
-
-        def more(i, carry):
-            for q in range(W8):
-                send_block(fs, fr, mb, i, q, 1, fs_sem, fr_sem)
-            return carry
-
-        lax.fori_loop(1, DEV // W8, more, 0)
-        return carry
-
-    lax.fori_loop(0, MB, send_rows, 0)
-
+    lax.fori_loop(0, MB, outgoing, 0)
+
+    for mb in range(MB):
+        list_of(MB + mb, -1, etgt_ref, mb)
+
+    def incoming(mb, carry):
+        for i in range(NCH):
+            wide, flat = expand(MB + mb, i)
+            rows = slice(i * EC, (i + 1) * EC)
+            tcolf[mb, rows, :] = wide
+            th[mb, rows, :] = onehot_rows(wide.astype(jnp.int32).astype(jnp.int16))
+            trow[mb, i] = flat
+        fill_turned(trow, mb, tht)
+        return carry
+
+    lax.fori_loop(0, MB, incoming, 0)
     for mb in range(MB):
         for i in range(N // 128):
             xt_v[mb, :, i * 128:(i + 1) * 128] = jnp.transpose(x_v[mb, i * 128:(i + 1) * 128, :])
@@ -335,8 +326,17 @@
         sweep_chunk(mb, NCH - 1)
 
     def tops(mb):
-        best = jnp.max(mx_v[...], axis=1)
-        best = jnp.concatenate([best, jnp.zeros((128 - 2 * groups, 128), F32)], axis=0)
+        tall = [mx_v[at] for at in range(2 * groups)]
+        for shift in (4, 2, 1):
+            tall = [jnp.maximum(v, pltpu.roll(v, shift, 0)) for v in tall]
+        sub = iota((8, 128), 0)
+        best = []
+        for at in range(0, 2 * groups, 8):
+            row = tall[at]
+            for k in range(1, min(8, 2 * groups - at)):
+                row = jnp.where(sub == k, tall[at + k], row)
+            best.append(row)
+        best = jnp.concatenate(best + [jnp.zeros((128 - 8 * len(best), 128), F32)], axis=0)
         turned = jnp.transpose(best)
         both = turned[0:64, :] + pltpu.roll(turned[64:128, :], 32, 1)
         hi = both.astype(BF).astype(F32)
@@ -422,21 +422,16 @@
         dz = ds * ga_v[rows, :]
         eg = (p * dag + dz).astype(BF)
         rs[mb, rows, :] = eg
-        gacc[:, 0:C] += dot_tn(fr[mb, rows, :], eg)
-        fr[mb, rows, :] = dz.astype(BF)
-
-    def return_chunk(mb, i):
-        if i == 0:
-            keep_block(rs, rr, mb, rr_sem)
-        for j in range(max(1, i * PER), (i + 1) * PER):
-            send_block(rs, rr, mb, j // W8, j % W8, -1, rs_sem, rr_sem)
+        fs[mb, rows, :] = dz.astype(BF)
 
     def backward_edges(mb):
         for i in range(NCH):
             grad_chunk(mb, i)
             if i > 0:
-                return_chunk(mb, i - 1)
-        return_chunk(mb, NCH - 1)
+                send_chunk(rs, rr, mb, i - 1, -1, rs_sem, rr_sem)
+        send_chunk(rs, rr, mb, NCH - 1, -1, rs_sem, rr_sem)
+
+    most = pl.ds(0, (DEV - 1) * CAP)
 
     def one_batch(mb, carry):
         forward_edges(mb)
@@ -444,6 +439,7 @@
         weigh(mb)
         nodes(mb)
         pltpu.make_async_copy(cot_v.at[mb], out_hbm.at[mb], out_sem.at[mb]).start()
+        pltpu.make_async_copy(fs.at[mb, most], fs.at[mb, most], fs_sem.at[mb]).wait()
         backward_edges(mb)
         return carry
 
@@ -452,9 +448,10 @@
     def local_grads(mb, carry):
         for i in range(N // NB):
             rows = slice(i * NB, (i + 1) * NB)
-            dtgt = dot(tht[mb, rows, :], fr[mb]) + loc_v[mb, rows, C:2 * C].astype(F32)
+            dtgt = dot(tht[mb, rows, :], fs[mb]) + loc_v[mb, rows, C:2 * C].astype(F32)
             loc_v[mb, rows, C:2 * C] = dtgt.astype(BF)
         gacc[...] += dot(xt_v[mb], loc_v[mb])
+        gacc[:, 0:C] += dot_tn(fr[mb], rs[mb])
         return carry
 
     lax.fori_loop(0, MB, local_grads, 0)
@@ -550,8 +547,6 @@
 
     for mb in range(MB):
         pltpu.make_async_copy(cot_v.at[mb], gf_hbm.at[mb], out_sem.at[mb]).wait()
-        most = pl.ds(0, (DEV - 1) * CAP)
-        pltpu.make_async_copy(fs.at[mb, most], fs.at[mb, most], fs_sem.at[mb]).wait()
         pltpu.make_async_copy(rs.at[mb, most], rs.at[mb, most], rs_sem.at[mb]).wait()
     pltpu.make_async_copy(mine, mine, w_sem.at[2]).wait()
     others = pl.ds(0, ND - 1)
@@ -604,7 +599,6 @@
     RW = C // ND
     PK = 3 * RW + 16
     groups = N // 64
-    TC = min(E, 256)
     vmem = pl.BlockSpec(memory_space=pltpu.VMEM)
     hbm = pl.BlockSpec(memory_space=pl.ANY)
     smem = pl.BlockSpec(memory_space=pltpu.SMEM)
@@ -624,8 +618,8 @@
             V((MB, N, C), BF), V((MB, C, N), BF), V((MB, N, C), BF),
             V((MB, E, C), BF), V((MB, E, C), BF), V((MB, E, C), BF), V((MB, E, C), BF),
             V((PK, C), BF), V((ND, PK, C), BF), V((C, 3 * C), BF),
-            V((MB, E, 128), F32),
-            V((MB, E // TC, 16, TC), I16), V((MB, E // TC, 16, TC), I16),
+            V((2 * MB, DEV, 2 * CAP), BF), V((MB, E, 128), F32),
+            V((MB, NCH, 16, EC), I16), V((MB, NCH, 16, EC), I16),
             V((MB, E, N), BF), V((MB, N, E), BF),
             V((E, C), BF), V((E, C), BF), V((E, C), F32), V((max(E, 2 * N), C), F32), V((E, 2 * C), BF),
             V((MB, N, C), BF), V((MB, N, C), BF), V((MB, N, C), F32),

time: 109 us -> 103 us (0.945)
  Pallas kernels: 108 us -> 102 us
    pallas_call x1, Pallas kernels: 104 us -> 98 us  [local(): pl.pallas_call(functools.partial(kernel, cfg), out_shape=(wide, wide, jax...]
where the time goes in v2:
time: 103 us
  Pallas kernels  102 us (99%)
    pallas_call x1, Pallas kernels, local(): pl.pallas_call(functools.partial(kernel, cfg), out_shape=(wide, wide, jax...  98 us
    pallas_call x1, Pallas kernels, local(): pl.pallas_call(functools.partial(hand_on, RW), out_shape=(wide, wide, blo...  3.89 us

profile of v2, /device:TPU:1, one launch (start us, length us, event | category | flops | bytes accessed | tf_op | source)
XLA Modules:
  0.0 102.8 jit_solution(12186845367733487763)
XLA Ops:
  0.6 98.0 %shard_map.187 = (bf16[2,1024,256]{2,1,0:T(8,128)(2,1)}, bf16[2,1024,256]{2,1,0:T(8,128)(2,1)}, f32[64,256]{1,0:T(8,128)}) custom-call(s32[1,2]{1,0:T(1,128)} %bitcast.13, s32[2,1,16,128]{3,2,1,0:T(8,128)} %bitcast.11, s32[2,1,16,128]{3,2,1,0:T(8,128)} %bitcast.12, bf16[1,16]{1,0:T(2,128)(2,1)} %bitcast.14, bf16[1,16]{1,0:T(2,128)(2,1)} %bitcast.15, ...), custom_call_target="tpu_custom_call" | custom-call | flops 21474836480 | bytes 5242880 | tf_op jit(solution)/shard_map/pallas_call | solution.py:612
  98.7 3.9 %shard_map.188 = (bf16[2,1024,256]{2,1,0:T(8,128)(2,1)}, bf16[2,1024,256]{2,1,0:T(8,128)(2,1)}, f32[16,256]{1,0:T(8,128)}, f32[16,256]{1,0:T(8,128)}, f32[16,256...) custom-call(bf16[2,1024,256]{2,1,0:T(8,128)(2,1)} %get-tuple-element.21.out_in, ...), custom_call_target="tpu_custom_call" | custom-call | tf_op jit(solution)/shard_map/pallas_call | solution.py:647

commit v3 on v2

--- a/solution.py
+++ b/solution.py
@@ -51,7 +51,7 @@
     cnt_ref, esrc_ref, etgt_ref, att_ref, bias_ref, gain_ref, shift_ref,
     x_hbm, cot_hbm, ws_hbm, wt_hbm, wr_hbm,
     out_hbm, gf_hbm, small_ref,
-    x_v, xt_v, cot_v, fs, fr, rs, rr, wsend, wall, wcat,
+    x_v, cot_v, fs, fr, rs, rr, wsend, wall, wcat,
     lists, tcolf, trow, srow, th, tht,
     se_v, g_v, ga_v, sc_v, pv_v, sp_v, tp_v, rp_v, sg_v, sga_v, ssc_v, mtab, mx_v,
     dtab, loc_v, a2, eblk, exp2, spread, sel, vecs, vacc, gacc,
@@ -69,6 +69,7 @@
     HALF = PK // 2
     NB = min(256, N)
     W8 = 2 * X
+    STEP = 1
     g, d = lax.axis_index("grp"), lax.axis_index("dev")
     mx, mc = lax.div(g, 2), lax.rem(g, 2)
     my, mz = lax.div(d, Z), lax.rem(d, Z)
@@ -91,19 +92,6 @@
             lax.rem(py, Y) * Z + lax.rem(pz, Z),
         )
 
-    barrier = pltpu.get_barrier_semaphore()
-
-    def greet(i, q):
-        pl.semaphore_signal(barrier, inc=1, device_id=place(i, q, 1), device_id_type=MESH)
-
-    def greet_all(i, carry):
-        for q in range(W8):
-            greet(i, q)
-        return carry
-
-    for q in range(1, W8):
-        greet(0, q)
-    lax.fori_loop(1, DEV // W8, greet_all, 0)
     loads = [
         pltpu.make_async_copy(x_hbm, x_v, in_sem.at[0]),
         pltpu.make_async_copy(ws_hbm, wsend.at[pl.ds(0, RW)], in_sem.at[1]),
@@ -114,6 +102,13 @@
     for load in loads:
         load.start()
 
+    barrier = pltpu.get_barrier_semaphore()
+
+    def greet(i, q):
+        pl.semaphore_signal(barrier, inc=1, device_id=place(i, q, 1), device_id_type=MESH)
+
+    for j in range(1, DEV):
+        greet(j // W8, j % W8)
     rep = (iota((RW, C), 1) % RW == iota((RW, C), 0)).astype(F32).astype(BF)
     here = (iota((8, C), 1) // RW == d)
     rows = [jnp.where(here, dot(jnp.broadcast_to(ref[...], (8, RW)), rep), 0.0)
@@ -232,10 +227,6 @@
         return carry
 
     lax.fori_loop(0, MB, incoming, 0)
-    for mb in range(MB):
-        for i in range(N // 128):
-            xt_v[mb, :, i * 128:(i + 1) * 128] = jnp.transpose(x_v[mb, i * 128:(i + 1) * 128, :])
-
     same = (iota((C, C), 0) // 64) == (iota((C, C), 1) // 64)
     eblk[...] = same.astype(F32).astype(BF)
     lane = iota((128, C), 0)
@@ -293,8 +284,6 @@
 
     def score_chunk(mb, i):
         rows = edge_rows(i)
-        part = fr.at[mb, pl.ds(i * EC, EC)]
-        pltpu.make_async_copy(part, part, fr_sem.at[mb, i]).wait()
         se = dot(fr[mb, rows, :], wcat[:, 0:C]).astype(BF)
         se_v[rows, :] = se
         z = se.astype(F32) + dot(th[mb, rows, :], tp_v[mb])
@@ -305,21 +294,25 @@
         sc_v[rows, :] = dot(hi, a2[...]) + dot(lo, a2[...])
 
     def sweep_chunk(mb, i):
-        low = (iota((128, 128), 1) & 63).astype(F32)
-        for q in range(EC // 128):
-            part = slice(i * EC + q * 128, i * EC + (q + 1) * 128)
+        low = (iota((64, 128), 1) & 63).astype(F32)
+        for q in range(EC // 64):
+            part = slice(i * EC + q * 64, i * EC + (q + 1) * 64)
             tgt = tcolf[mb, part, :]
             s0, s1 = sc_v[part, 0:128], sc_v[part, 128:256]
             for grp in range(groups):
                 hit = tgt == low + (64.0 * grp)
                 for side, s in enumerate((s0, s1)):
-                    top = jnp.max(jnp.where(hit, s, LOWEST).reshape(16, 8, 128), axis=0)
+                    top = jnp.max(jnp.where(hit, s, LOWEST).reshape(8, 8, 128), axis=0)
                     at = side * groups + grp
                     mx_v[at] = jnp.maximum(mx_v[at], top)
 
     def forward_edges(mb):
         mx_v[...] = jnp.full(mx_v.shape, LOWEST, F32)
         for i in range(NCH):
+            if i % STEP == 0:
+                for k in range(i, min(i + STEP, NCH)):
+                    part = fr.at[mb, pl.ds(k * EC, EC)]
+                    pltpu.make_async_copy(part, part, fr_sem.at[mb, k]).wait()
             score_chunk(mb, i)
             if i > 0:
                 sweep_chunk(mb, i - 1)
@@ -358,14 +351,14 @@
             live = tcolf[mb, rows, :] >= 0.0
             live = jnp.concatenate([live, live], axis=1)
             p = jnp.where(live, jnp.exp(sc_v[rows, :] - dot(me, exp2[...])), 0.0)
-            pv_v[rows, 0:C] = (p * se_v[rows, :].astype(F32)).astype(BF)
-            pv_v[rows, C:2 * C] = p.astype(BF)
+            rs[mb, rows, :] = (p * se_v[rows, :].astype(F32)).astype(BF)
+            pv_v[rows, :] = p.astype(BF)
 
     def nodes(mb):
         for i in range(N // NB):
             rows = slice(i * NB, (i + 1) * NB)
-            sc_v[rows, :] = dot(tht[mb, rows, :], pv_v[:, 0:C])
-            sc_v[N + i * NB:N + (i + 1) * NB, :] = dot(tht[mb, rows, :], pv_v[:, C:2 * C])
+            sc_v[rows, :] = dot(tht[mb, rows, :], rs[mb])
+            sc_v[N + i * NB:N + (i + 1) * NB, :] = dot(tht[mb, rows, :], pv_v[...])
         for i in range(N // NB):
             r = i * NB
             rows = slice(r, r + NB)
@@ -416,7 +409,7 @@
         dag = got[:, 0:C]
         se = se_v[rows, :].astype(F32)
         hi, lo = split(dag * se)
-        p = pv_v[rows, C:2 * C].astype(F32)
+        p = pv_v[rows, :].astype(F32)
         ds = p * (dot(hi, eblk[...]) + dot(lo, eblk[...]) - dot(got[:, C:C + 128].astype(BF), exp2[...]))
         vacc[0] += fold(ds * g_v[rows, :].astype(F32))
         dz = ds * ga_v[rows, :]
@@ -450,7 +443,7 @@
             rows = slice(i * NB, (i + 1) * NB)
             dtgt = dot(tht[mb, rows, :], fs[mb]) + loc_v[mb, rows, C:2 * C].astype(F32)
             loc_v[mb, rows, C:2 * C] = dtgt.astype(BF)
-        gacc[...] += dot(xt_v[mb], loc_v[mb])
+        gacc[...] += dot_tn(x_v[mb], loc_v[mb])
         gacc[:, 0:C] += dot_tn(fr[mb], rs[mb])
         return carry
 
@@ -615,13 +608,13 @@
         in_specs=[smem] + [vmem] * 6 + [hbm] * 5,
         out_specs=(hbm, hbm, vmem),
         scratch_shapes=[
-            V((MB, N, C), BF), V((MB, C, N), BF), V((MB, N, C), BF),
+            V((MB, N, C), BF), V((MB, N, C), BF),
             V((MB, E, C), BF), V((MB, E, C), BF), V((MB, E, C), BF), V((MB, E, C), BF),
             V((PK, C), BF), V((ND, PK, C), BF), V((C, 3 * C), BF),
             V((2 * MB, DEV, 2 * CAP), BF), V((MB, E, 128), F32),
             V((MB, NCH, 16, EC), I16), V((MB, NCH, 16, EC), I16),
             V((MB, E, N), BF), V((MB, N, E), BF),
-            V((E, C), BF), V((E, C), BF), V((E, C), F32), V((max(E, 2 * N), C), F32), V((E, 2 * C), BF),
+            V((E, C), BF), V((E, C), BF), V((E, C), F32), V((max(E, 2 * N), C), F32), V((E, C), BF),
             V((MB, N, C), BF), V((MB, N, C), BF), V((MB, N, C), F32),
             V((MB, N, C), BF), V((MB, N, C), F32), V((MB, N, C), F32),
             V((N, 128), BF), V((2 * groups, 8, 128), F32),

time: 103 us -> 103 us (level)
  no operation moved by 1% of the time
where the time goes in v3:
time: 103 us
  Pallas kernels  102 us (99%)
    pallas_call x1, Pallas kernels, local(): pl.pallas_call(functools.partial(kernel, cfg), out_shape=(wide, wide, jax...  97.8 us
    pallas_call x1, Pallas kernels, local(): pl.pallas_call(functools.partial(hand_on, RW), out_shape=(wide, wide, blo...  3.89 us

profile of v3, /device:TPU:1, one launch (start us, length us, event | category | flops | bytes accessed | tf_op | source)
XLA Modules:
  0.0 102.5 jit_solution(14833178727917442205)
XLA Ops:
  0.6 97.8 %shard_map.187 = (bf16[2,1024,256]{2,1,0:T(8,128)(2,1)}, bf16[2,1024,256]{2,1,0:T(8,128)(2,1)}, f32[64,256]{1,0:T(8,128)}) custom-call(s32[1,2]{1,0:T(1,128)} %bitcast.13, s32[2,1,16,128]{3,2,1,0:T(8,128)} %bitcast.11, s32[2,1,16,128]{3,2,1,0:T(8,128)} %bitcast.12, bf16[1,16]{1,0:T(2,128)(2,1)} %bitcast.14, bf16[1,16]{1,0:T(2,128)(2,1)} %bitcast.15, ...), custom_call_target="tpu_custom_call" | custom-call | flops 21474836480 | bytes 5242880 | tf_op jit(solution)/shard_map/pallas_call | solution.py:605
  98.4 3.9 %shard_map.188 = (bf16[2,1024,256]{2,1,0:T(8,128)(2,1)}, bf16[2,1024,256]{2,1,0:T(8,128)(2,1)}, f32[16,256]{1,0:T(8,128)}, f32[16,256]{1,0:T(8,128)}, f32[16,256...) custom-call(bf16[2,1024,256]{2,1,0:T(8,128)(2,1)} %get-tuple-element.21.out_in, ...), custom_call_target="tpu_custom_call" | custom-call | tf_op jit(solution)/shard_map/pallas_call | solution.py:640

commit v4 on v3

--- a/solution.py
+++ b/solution.py
@@ -211,7 +211,16 @@
     lax.fori_loop(1, ND, send_weights, 0)
     pltpu.make_async_copy(wsend.at[half], wall.at[d, half], w_sem.at[1]).start()
 
-    lax.fori_loop(0, MB, outgoing, 0)
+    outgoing(0, 0)
+
+    mine = wall.at[:, half]
+    pltpu.make_async_copy(mine, mine, w_sem.at[1]).wait()
+    pltpu.make_async_remote_copy(
+        src_ref=mine, dst_ref=mine, send_sem=w_sem.at[2], recv_sem=w_sem.at[3],
+        device_id=twin, device_id_type=MESH,
+    ).start()
+    for mb in range(1, MB):
+        outgoing(mb, 0)
 
     for mb in range(MB):
         list_of(MB + mb, -1, etgt_ref, mb)
@@ -243,12 +252,6 @@
     vacc[...] = jnp.zeros_like(vacc)
     gacc[...] = jnp.zeros_like(gacc)
 
-    mine = wall.at[:, half]
-    pltpu.make_async_copy(mine, mine, w_sem.at[1]).wait()
-    pltpu.make_async_remote_copy(
-        src_ref=mine, dst_ref=mine, send_sem=w_sem.at[2], recv_sem=w_sem.at[3],
-        device_id=twin, device_id_type=MESH,
-    ).start()
     pltpu.make_async_copy(mine, mine, w_sem.at[3]).wait()
     for slot in range(3):
         wcat[:, slot * C:(slot + 1) * C] = wall[:, slot * RW:(slot + 1) * RW, :].reshape(C, C)

time: 103 us -> 106 us (1.029)
  Pallas kernels: 102 us -> 105 us
    pallas_call x1, Pallas kernels: 97.8 us -> 101 us  [local(): pl.pallas_call(functools.partial(kernel, cfg), out_shape=(wide, wide, jax...]
where the time goes in v4:
time: 106 us
  Pallas kernels  105 us (99%)
    pallas_call x1, Pallas kernels, local(): pl.pallas_call(functools.partial(kernel, cfg), out_shape=(wide, wide, jax...  101 us
    pallas_call x1, Pallas kernels, local(): pl.pallas_call(functools.partial(hand_on, RW), out_shape=(wide, wide, blo...  3.89 us

profile of v4, /device:TPU:1, one launch (start us, length us, event | category | flops | bytes accessed | tf_op | source)
XLA Modules:
  0.0 105.8 jit_solution(10936177610595499973)
XLA Ops:
  0.6 101.1 %shard_map.187 = (bf16[2,1024,256]{2,1,0:T(8,128)(2,1)}, bf16[2,1024,256]{2,1,0:T(8,128)(2,1)}, f32[64,256]{1,0:T(8,128)}) custom-call(s32[1,2]{1,0:T(1,128)} %bitcast.13, s32[2,1,16,128]{3,2,1,0:T(8,128)} %bitcast.11, s32[2,1,16,128]{3,2,1,0:T(8,128)} %bitcast.12, bf16[1,16]{1,0:T(2,128)(2,1)} %bitcast.14, bf16[1,16]{1,0:T(2,128)(2,1)} %bitcast.15, ...), custom_call_target="tpu_custom_call" | custom-call | flops 21474836480 | bytes 5242880 | tf_op jit(solution)/shard_map/pallas_call | solution.py:608
  101.8 3.9 %shard_map.188 = (bf16[2,1024,256]{2,1,0:T(8,128)(2,1)}, bf16[2,1024,256]{2,1,0:T(8,128)(2,1)}, f32[16,256]{1,0:T(8,128)}, f32[16,256]{1,0:T(8,128)}, f32[16,256...) custom-call(bf16[2,1024,256]{2,1,0:T(8,128)(2,1)} %get-tuple-element.21.out_in, ...), custom_call_target="tpu_custom_call" | custom-call | tf_op jit(solution)/shard_map/pallas_call | solution.py:643
